TPU v7x, 32 devices: a whole 2x2x4 slice. The times are simulated.
32 devices in a mesh: box: 8 (over y, x, core), slab: 4 (over z).
Axes of the slice: x: 2, y: 2, z: 4, core: 2. Of those that a mesh axis runs over, the one named last changes fastest.
Arguments:
- velocity: bfloat16 [8, 3, 8, 16, 64, 128], P('box', None, None, None, 'slab'), may hold values from -6 to 6
- field: float32 [8, 3, 8, 16, 64], P('box', None, None, None, 'slab'), may hold values from -6 to 6
- conductivity: float32 [8, 8, 16, 64], P('box', None, None, 'slab'), may hold values from 0.5 to 2
- wall_flags: int32 [8, 8, 16, 64], P('box', None, None, 'slab'), may hold values 0 or 1
- leaf_solution: bfloat16 [8, 4, 512, 2048], P('box', 'slab'), may hold values from -0.125 to 0.125
- leaf_dtn: float32 [8, 4, 512, 512], P('box', 'slab'), as said below
Outputs:
- interface_two: float32 [8, 4, 256, 128], P('box', 'slab')
- neumann_two: float32 [8, 4, 512, 128], P('box', 'slab')
Inputs may be any that keep to these rules, and one draw needn't show every extreme that they name: `leaf_dtn`: every leaf map is symmetric positive definite.
All inputs are finite; a program needn't handle non-finite values. No bound on the sum of `wall_flags` on one device may be relied on, other than what follows from the above.
Results may differ from a plain program's by a relative error of at most 0.0029.
Values sent between devices are 32-bit elements; how exact they have to be, the bound alone decides.
A program may use at most 64 MiB of HBM per device.

v0:
```python
import functools

import jax
import jax.numpy as jnp
from jax import lax
from jax.experimental import pallas as pl
from jax.experimental.pallas import tpu as pltpu
from jax.sharding import PartitionSpec as P

WALL_RATIO = 8.0
SQUARINGS = 3
NEWTON_LIMIT = 12
CLOSE = 0.05
VMEM = pl.BlockSpec(memory_space=pltpu.VMEM)


def dot1(a, b):
    return jnp.dot(
        a.astype(jnp.bfloat16), b.astype(jnp.bfloat16), preferred_element_type=jnp.float32
    )


def halves(a):
    high = a.astype(jnp.bfloat16)
    return high, (a - high.astype(jnp.float32)).astype(jnp.bfloat16)


def dot3(a, b):
    ah, al = halves(a)
    bh, bl = halves(b)
    return dot1(ah, bh) + (dot1(ah, bl) + dot1(al, bh))


def eye(width):
    rows = lax.broadcasted_iota(jnp.int32, (width, width), 0)
    columns = lax.broadcasted_iota(jnp.int32, (width, width), 1)
    return (rows == columns).astype(jnp.float32)


def approximate_inverse(schur, inverse):
    width = schur.shape[0]
    unit = eye(width)
    matrix = schur[...]
    scale = jnp.sum(unit * matrix) / jnp.sum(matrix * matrix)
    power = unit - scale * matrix
    total = unit + power
    for _ in range(SQUARINGS):
        power = dot1(power, power)
        total = total + dot1(total, power)
    inverse[...] = scale * total

    def error():
        return unit - dot3(schur[...], inverse[...])

    first = error()

    def body(state):
        step, residual, norm = state
        inverse[...] += dot3(inverse[...], residual)
        residual = error()
        return step + 1, residual, jnp.sum(residual * residual)

    def far(state):
        step, residual, norm = state
        return jnp.logical_and(step < NEWTON_LIMIT, jnp.logical_not(norm < CLOSE * CLOSE))

    step, residual, norm = lax.while_loop(far, body, (0, first, jnp.sum(first * first)))
    good = norm < CLOSE * CLOSE

    @pl.when(good)
    def _():
        inverse[...] += dot1(inverse[...], residual)

    @pl.when(jnp.logical_not(good))
    def _():
        inverse[...] = schur[...]
        lane = lax.broadcasted_iota(jnp.int32, (width, width), 1)
        sublane = lax.broadcasted_iota(jnp.int32, (width, width), 0)

        def eliminate(k, carry):
            m = inverse[...]
            at = lane == k
            row = jnp.sum(jnp.where(sublane == k, m, 0.0), axis=0, keepdims=True)
            column = jnp.sum(jnp.where(at, m, 0.0), axis=1, keepdims=True)
            at_row = lax.broadcasted_iota(jnp.int32, (1, width), 1) == k
            pivot = jnp.sum(jnp.where(at_row, row, 0.0), axis=1, keepdims=True)
            scaled = jnp.where(at_row, 1.0, row) / pivot
            inverse[...] = jnp.where(sublane == k, scaled, jnp.where(at, 0.0, m) - column * scaled)
            return carry

        lax.fori_loop(0, width, eliminate, 0)


def solve(schur, inverse, b):
    y = dot1(inverse, b)
    return y + dot1(inverse, b - dot3(schur, y))


def roles():
    box = lax.axis_index("box")
    low, high = lax.rem(box, 2), lax.rem(lax.div(box, 2), 2)
    return low, low != high


def block(ref, row, column):
    width = ref.shape[0] // 2
    r = pl.multiple_of(row * width, width)
    c = pl.multiple_of(column * width, width)
    return ref[pl.ds(r, width), pl.ds(c, width)]


def face(ref, at):
    width = ref.shape[0] // 2
    return ref[pl.ds(pl.multiple_of(at * width, width), width), :]


def map_kernel(own, other, schur, inverse, parent, outward):
    low, inner = roles()
    mine, theirs = 1 - low, low
    schur[...] = block(own, mine, mine) + block(other, theirs, theirs)
    approximate_inverse(schur, inverse)
    inner_mi = jnp.where(inner, block(own, mine, low), block(other, theirs, mine))
    inner_im = jnp.where(inner, block(own, low, mine), block(other, mine, theirs))
    inner_ii = jnp.where(inner, block(own, low, low), block(other, mine, mine))
    outer_om = jnp.where(inner, block(other, mine, theirs), block(own, low, mine))
    weights = solve(schur[...], inverse[...], inner_mi)
    parent[...] = inner_ii - dot3(inner_im, weights)
    outward[...] = dot3(outer_om, weights)


def data_kernel(own, other, data, other_data, schur, inverse, inner_data, outer_data):
    low, inner = roles()
    mine, theirs = 1 - low, low
    b = face(data, mine) + face(other_data, theirs)
    interface = solve(schur[...], inverse[...], b)
    inner_im = jnp.where(inner, block(own, low, mine), block(other, mine, theirs))
    outer_om = jnp.where(inner, block(other, mine, theirs), block(own, low, mine))
    a, c = face(data, low), face(other_data, mine)
    inner_data[...] = jnp.where(inner, a, c) - dot3(inner_im, interface)
    outer_data[...] = jnp.where(inner, c, a) - dot3(outer_om, interface)


def second_map_kernel(parent, other_parent, schur, inverse):
    schur[...] = parent[...] + other_parent[...]
    approximate_inverse(schur, inverse)


def second_data_kernel(data, other_data, schur, inverse, outward, outer_data, interface, parent_data):
    y = solve(schur[...], inverse[...], data[...] + other_data[...])
    interface[...] = -y
    parent_data[...] = outer_data[...] + dot3(outward[...], y)


def local(kernel, outs, flops, *args):
    moved = sum(a.size * a.dtype.itemsize for a in args)
    return pl.pallas_call(
        kernel,
        out_shape=[jax.ShapeDtypeStruct(s, jnp.float32) for s in outs],
        in_specs=[VMEM] * len(args),
        out_specs=[VMEM] * len(outs),
        compiler_params=pltpu.CompilerParams(vmem_limit_bytes=32 * 1024 * 1024),
        cost_estimate=pl.CostEstimate(flops=flops, bytes_accessed=moved, transcendentals=0),
    )(*args)


def from_partner(block, axis, stride):
    count = lax.axis_size(axis)
    route = []
    for low in range(count):
        high = low | 1 << stride
        if high != low and high < count:
            route += [(low, high), (high, low)]
    return lax.ppermute(block, axis, route)


def padded_2(block, sides, width):
    for axis, dim in sides:
        count = lax.axis_size(axis)
        forward = [(i, i + 1) for i in range(count - 1)]
        backward = [(target, source) for source, target in forward]
        low = lax.ppermute(
            lax.slice_in_dim(block, block.shape[dim] - width, None, axis=dim), axis, forward
        )
        high = lax.ppermute(lax.slice_in_dim(block, 0, width, axis=dim), axis, backward)
        block = jnp.concatenate([low, block, high], axis=dim)
    return block


def currents(velocity, field, conductivity, wall_flags):
    sigma = conductivity * jnp.where(wall_flags == 1, WALL_RATIO, 1.0).astype(conductivity.dtype)
    speed = velocity.astype(jnp.float32)
    magnet = field[..., None]
    weight = sigma[..., None]
    elec_x = speed[1] * magnet[2] - speed[2] * magnet[1]
    elec_y = speed[2] * magnet[0] - speed[0] * magnet[2]
    elec_z = speed[0] * magnet[1] - speed[1] * magnet[0]
    return (weight * elec_x, weight * elec_y, weight * elec_z)


def divergence(flow_x, flow_y, padded_z):
    padded_x = jnp.pad(flow_x, ((1, 1), (0, 0), (0, 0), (0, 0)))
    padded_y = jnp.pad(flow_y, ((0, 0), (1, 1), (0, 0), (0, 0)))
    return 0.5 * (
        padded_x[2:]
        - padded_x[:-2]
        + (padded_y[:, 2:] - padded_y[:, :-2])
        + (padded_z[:, :, 2:] - padded_z[:, :, :-2])
    )


def on_device(velocity, field, conductivity, wall_flags, leaf_solution, leaf_dtn):
    dtn_map = leaf_dtn[0, 0]
    width = dtn_map.shape[0] // 2
    square = (width, width)
    other_map = from_partner(dtn_map, "box", 0)
    flow_x, flow_y, flow_z = currents(velocity[0], field[0], conductivity[0], wall_flags[0])
    solution_map = leaf_solution[0, 0]
    sizex, sizey, depth, snaps = flow_x.shape
    thin = (width, snaps)
    cell_count = sizex * sizey * depth
    padded = padded_2(flow_z, (("slab", 2),), 1)
    source = divergence(flow_x, flow_y, padded).astype(jnp.bfloat16)
    neumann = jnp.dot(
        solution_map, source.reshape(cell_count, snaps), preferred_element_type=jnp.float32
    )
    other_neumann = from_partner(neumann, "box", 0)

    cube = 2 * width**3
    schur, inverse, parent, outward = local(
        map_kernel, [square] * 4, 30 * cube, dtn_map, other_map
    )
    other_parent = from_partner(parent, "box", 1)
    schur_two, inverse_two = local(
        second_map_kernel, [square] * 2, 20 * cube, parent, other_parent
    )
    inner_data, outer_data = local(
        data_kernel, [thin] * 2, 6 * cube, dtn_map, other_map, neumann, other_neumann, schur, inverse
    )
    other_inner = from_partner(inner_data, "box", 1)
    interface, own_side = local(
        second_data_kernel,
        [thin] * 2,
        4 * cube,
        inner_data,
        other_inner,
        schur_two,
        inverse_two,
        outward,
        outer_data,
    )
    other_side = from_partner(own_side, "box", 1)
    left = lax.axis_index("box") >> 1 & 1 == 0
    first = jnp.where(left, own_side, other_side)
    second = jnp.where(left, other_side, own_side)
    return (interface[None, None], jnp.concatenate([first, second], axis=0)[None, None])


def solution(mesh):
    return jax.shard_map(
        on_device,
        mesh=mesh,
        in_specs=(
            P("box", None, None, None, "slab", None),
            P("box", None, None, None, "slab"),
            P("box", None, None, "slab"),
            P("box", None, None, "slab"),
            P("box", "slab", None, None),
            P("box", "slab", None, None),
        ),
        out_specs=(P("box", "slab", None, None), P("box", "slab", None, None)),
        check_vma=False,
    )
```

profile of v0, /device:TPU:0, one launch (start us, length us, event | category | flops | bytes accessed | tf_op | source)
XLA Modules:
  0.0 37.8 jit_solution(13130391178463382710)
XLA Ops:
  0.6 0.0 copy-start
  0.6 0.5 %collective-permute-start = (f32[512,512]{1,0:T(8,128)}, f32[512,512]{1,0:T(8,128)S(1)}, u32[]{:S(2)}, u32[]{:S(2)}) collective-permute-start(f32[512,512]{1,0:T(8,128)} %bitcast.39), channel_id=1, source_target_pairs={{0,4},{4,0},{8,12},{12,8},{16,20},{20,16},{24,28},{28,24},{1,5},{5... | collective-permute-start | bytes 3145736 | tf_op jit(solution)/shard_map/ppermute | solution.py:173
  1.2 1.0 %slice_bitcast_fusion.4 = (f32[8,16,16]{2,1,0:T(8,128)S(1)}, f32[8,16,16]{2,1,0:T(8,128)S(1)}, f32[8,16,16]{2,1,0:T(8,128)S(1)}) fusion(f32[1,3,8,16,16]{4,3,2,1,0:T(8,128)} %param.7), kind=kLoop, calls=%fused_computation.24 | loop fusion | bytes 49152 | tf_op jit(solution)/shard_map/mul | solution.py:194
  2.2 0.0 copy-start.2
  2.2 0.0 copy-start.3
  2.2 1.8 %convert_element_type.11 = f32[1,3,8,16,16,128]{5,4,3,2,1,0:T(8,128)S(1)} convert(bf16[1,3,8,16,16,128]{5,4,3,2,1,0:T(8,128)(2,1)} %param.6) | non-fusion elementwise | flops 786432 | bytes 4718592 | tf_op jit(solution)/shard_map/convert_element_type | solution.py:191
  4.0 0.0 copy-done.2
  4.0 0.0 copy-done.3
  4.0 1.4 %subtract_multiply_fusion = (f32[8,16,16,128]{3,2,1,0:T(8,128)S(1)}, f32[8,16,16,128]{3,2,1,0:T(8,128)S(1)}, f32[8,16,16,128]{3,2,1,0:T(8,128)S(1)}) fusion(f32[1,3,8,16,16,128]{5,4,3,2,1,0:T(8,128)S(1)} %convert_element_type.11, f32[8,16,16]{2,1,0:T(8,128)S(1)} %get-tuple-element.31, f32[8,16,16]{2,1,0:T(8,128)S(1)} %get-tuple-element.29, ...), kind=kLoop, calls=%fused_computation.19 | loop fusion | flops 3145728 | bytes 6324224 | tf_op jit(solution)/shard_map/mul | solution.py:197
  5.5 0.1 fusion.12
  5.6 1.3 %collective-permute-start.1 = (f32[8,16,1,128]{3,2,1,0:T(1,128)S(1)}, f32[8,16,1,128]{3,2,1,0:T(1,128)S(1)}, u32[]{:S(2)}, u32[]{:S(2)}) collective-permute-start(f32[8,16,1,128]{3,2,1,0:T(1,128)S(1)} %get-tuple-element.25), channel_id=1, source_target_pairs={{1,0},{2,1},{3,2},{5,4},{6,5},{7,6},{9,8},{10,9},{11,10},{13,12},{... | collective-permute-start | bytes 196616 | tf_op jit(solution)/shard_map/ppermute | solution.py:184
  6.9 5.2 %collective-permute-start.2 = (f32[8,16,1,128]{3,2,1,0:T(1,128)S(1)}, f32[8,16,1,128]{3,2,1,0:T(1,128)S(1)}, u32[]{:S(2)}, u32[]{:S(2)}) collective-permute-start(f32[8,16,1,128]{3,2,1,0:T(1,128)S(1)} %get-tuple-element.26), channel_id=1, source_target_pairs={{0,1},{1,2},{2,3},{4,5},{5,6},{6,7},{8,9},{9,10},{10,11},{12,13},{... | collective-permute-start | bytes 196616 | tf_op jit(solution)/shard_map/ppermute | solution.py:181
  12.0 0.7 %collective-permute-done.1 = f32[8,16,1,128]{3,2,1,0:T(1,128)S(1)} collective-permute-done((f32[8,16,1,128]{3,2,1,0:T(1,128)S(1)}, f32[8,16,1,128]{3,2,1,0:T(1,128)S(1)}, u32[]{:S(2)}, u32[]{:S(2)}) %collective-permute-start.1) | collective-permute-done | bytes 65568 | tf_op jit(solution)/shard_map/ppermute | solution.py:184
  12.7 1.2 %collective-permute-done.2 = f32[8,16,1,128]{3,2,1,0:T(1,128)S(1)} collective-permute-done((f32[8,16,1,128]{3,2,1,0:T(1,128)S(1)}, f32[8,16,1,128]{3,2,1,0:T(1,128)S(1)}, u32[]{:S(2)}, u32[]{:S(2)}) %collective-permute-start.2) | collective-permute-done | bytes 65568 | tf_op jit(solution)/shard_map/ppermute | solution.py:181
  13.9 0.5 %fusion.9 = bf16[8,16,16,128]{3,2,1,0:T(8,128)(2,1)S(1)} fusion(f32[8,16,16,128]{3,2,1,0:T(8,128)S(1)} %get-tuple-element.23, f32[8,16,16,128]{3,2,1,0:T(8,128)S(1)} %get-tuple-element.24, f32[8,16,16,128]{3,2,1,0:T(8,128)S(1)} %get-tuple-element.22, f32[8,16,1,128]{3,2,1,0:T(1,128)S(1)} %collective-permute-done.2, ...), kind=kLoop, calls=%fused_computation.11 | loop fusion | flops 2359296 | bytes 3801088 | tf_op jit(solution)/shard_map/convert_element_type | solution.py:222
  14.4 0.0 copy-start.1
  14.4 0.0 copy-done
  14.4 0.7 %fusion.2.data = f32[512,128]{1,0:T(8,128)S(1)} fusion(bf16[2048,128]{1,0:T(8,128)(2,1)S(1)} %bitcast.42, bf16[1,1,512,2048]{3,2,1,0:T(8,128)(2,1)S(1)} %copy-done), kind=kOutput, calls=%fused_computation.6 | convolution fusion | flops 268435456 | bytes 2883584 | tf_op jit(solution)/shard_map/dot_general | solution.py:223
  15.2 0.1 collective-permute-start.3
  15.2 0.0 collective-permute-done.other
  15.3 0.4 %copy-done.1 = f32[1,1,512,512]{3,2,1,0:T(8,128)S(1)} copy-done((f32[1,1,512,512]{3,2,1,0:T(8,128)S(1)}, f32[1,1,512,512]{3,2,1,0:T(8,128)}, u32[]{:S(2)}) %copy-start.1) | copy-done | bytes 1048600
  15.7 2.8 %shard_map.77 = (f32[256,256]{1,0:T(8,128)S(1)}, f32[256,256]{1,0:T(8,128)S(1)}, f32[256,256]{1,0:T(8,128)S(1)}, f32[256,256]{1,0:T(8,128)S(1)}) custom-call(f32[512,512]{1,0:T(8,128)S(1)} %bitcast.40, f32[512,512]{1,0:T(8,128)S(1)} %collective-permute-done.other), custom_call_target="tpu_custom_call" | custom-call | flops 1006632960 | bytes 2097152 | tf_op jit(solution)/shard_map/pallas_call | solution.py:156
  18.5 2.8 %collective-permute-start.5 = (f32[256,256]{1,0:T(8,128)S(1)}, f32[256,256]{1,0:T(8,128)S(1)}, u32[]{:S(2)}, u32[]{:S(2)}) collective-permute-start(f32[256,256]{1,0:T(8,128)S(1)} %get-tuple-element.15.parent), channel_id=1, source_target_pairs={{0,8},{8,0},{4,12},{12,4},{16,24},{24,16},{20,28},{28,20},{1,9},{9... | collective-permute-start | bytes 786440 | tf_op jit(solution)/shard_map/ppermute | solution.py:173
  21.3 0.0 collective-permute-done.3.other_data
  21.3 1.0 %shard_map.78 = (f32[256,128]{1,0:T(8,128)S(1)}, f32[256,128]{1,0:T(8,128)S(1)}) custom-call(f32[512,512]{1,0:T(8,128)S(1)} %bitcast.41, f32[512,512]{1,0:T(8,128)S(1)} %collective-permute-done.other, f32[512,128]{1,0:T(8,128)S(1)} %fusion.2.data, f32[512,128]{1,0:T(8,128)S(1)} %collective-permute-done.3.other_data, f32[256,256]{1,0:T(8,128)S(1)} %get-tuple-element.12.schur, ...), custom_call_target="tpu_custom_call" | custom-call | flops 201326592 | bytes 3145728 | tf_op jit(solution)/shard_map/pallas_call | solution.py:156
  22.3 0.1 collective-permute-start.4
  22.4 6.0 %collective-permute-done.5.other_parent = f32[256,256]{1,0:T(8,128)S(1)} collective-permute-done((f32[256,256]{1,0:T(8,128)S(1)}, f32[256,256]{1,0:T(8,128)S(1)}, u32[]{:S(2)}, u32[]{:S(2)}) %collective-permute-start.5) | collective-permute-done | bytes 262176 | tf_op jit(solution)/shard_map/ppermute | solution.py:173
  28.4 1.7 %shard_map.79 = (f32[256,256]{1,0:T(8,128)S(1)}, f32[256,256]{1,0:T(8,128)S(1)}) custom-call(f32[256,256]{1,0:T(8,128)S(1)} %get-tuple-element.15.parent, f32[256,256]{1,0:T(8,128)S(1)} %collective-permute-done.5.other_parent), custom_call_target="tpu_custom_call" | custom-call | flops 671088640 | bytes 524288 | tf_op jit(solution)/shard_map/pallas_call | solution.py:156
  30.1 0.5 %collective-permute-done.4.other_data = f32[256,128]{1,0:T(8,128)S(1)} collective-permute-done((f32[256,128]{1,0:T(8,128)S(1)}, f32[256,128]{1,0:T(8,128)S(1)}, u32[]{:S(2)}, u32[]{:S(2)}) %collective-permute-start.4) | collective-permute-done | bytes 131104 | tf_op jit(solution)/shard_map/ppermute | solution.py:173
  30.7 1.4 %shard_map.80 = (f32[256,128]{1,0:T(8,128)}, f32[256,128]{1,0:T(8,128)S(1)}) custom-call(f32[256,128]{1,0:T(8,128)S(1)} %get-tuple-element.14.data, f32[256,128]{1,0:T(8,128)S(1)} %collective-permute-done.4.other_data, f32[256,256]{1,0:T(8,128)S(1)} %get-tuple-element.16.schur, f32[256,256]{1,0:T(8,128)S(1)} %get-tuple-element.17.inverse, ...), custom_call_target="tpu_custom_call" | custom-call | flops 134217728 | bytes 1179648 | tf_op jit(solution)/shard_map/pallas_call | solution.py:156
  32.0 1.7 %collective-permute-start.6 = (f32[256,128]{1,0:T(8,128)S(1)}, f32[256,128]{1,0:T(8,128)S(1)}, u32[]{:S(2)}, u32[]{:S(2)}) collective-permute-start(f32[256,128]{1,0:T(8,128)S(1)} %get-tuple-element.21), channel_id=1, source_target_pairs={{0,8},{8,0},{4,12},{12,4},{16,24},{24,16},{20,28},{28,20},{1,9},{9... | collective-permute-start | bytes 393224 | tf_op jit(solution)/shard_map/ppermute | solution.py:173
  33.8 3.2 %collective-permute-done.6 = f32[256,128]{1,0:T(8,128)S(1)} collective-permute-done((f32[256,128]{1,0:T(8,128)S(1)}, f32[256,128]{1,0:T(8,128)S(1)}, u32[]{:S(2)}, u32[]{:S(2)}) %collective-permute-start.6) | collective-permute-done | bytes 131104 | tf_op jit(solution)/shard_map/ppermute | solution.py:173
  37.0 0.7 %maximum_bitcast_fusion = f32[1,1,512,128]{3,2,1,0:T(8,128)} fusion(f32[256,128]{1,0:T(8,128)S(1)} %get-tuple-element.28, f32[256,128]{1,0:T(8,128)S(1)} %get-tuple-element.27), kind=kLoop, calls=%fused_computation.22 | loop fusion | flops 65536 | bytes 524288 | tf_op jit(solution)/shard_map/broadcast_in_dim | solution.py:255
  (2 shorter events, 0.0 us)
Async XLA Ops:
  0.6 13.8 %copy-start = (bf16[1,1,512,2048]{3,2,1,0:T(8,128)(2,1)S(1)}, bf16[1,1,512,2048]{3,2,1,0:T(8,128)(2,1)}, u32[]{:S(2)}) copy-start(bf16[1,1,512,2048]{3,2,1,0:T(8,128)(2,1)} %param.10) | copy-start | bytes 6291460
  0.6 14.6 %collective-permute-start = (f32[512,512]{1,0:T(8,128)}, f32[512,512]{1,0:T(8,128)S(1)}, u32[]{:S(2)}, u32[]{:S(2)}) collective-permute-start(f32[512,512]{1,0:T(8,128)} %bitcast.39), channel_id=1, source_target_pairs={{0,4},{4,0},{8,12},{12,8},{16,20},{20,16},{24,28},{28,24},{1,5},{5... | collective-permute-start | bytes 3145736 | tf_op jit(solution)/shard_map/ppermute | solution.py:173
  2.2 1.8 %copy-start.2 = (f32[1,8,16,16]{3,2,1,0:T(8,128)S(1)}, f32[1,8,16,16]{3,2,1,0:T(8,128)}, u32[]{:S(2)}) copy-start(f32[1,8,16,16]{3,2,1,0:T(8,128)} %param.8) | copy-start | bytes 24580
  2.2 1.8 %copy-start.3 = (s32[1,8,16,16]{3,2,1,0:T(8,128)S(1)}, s32[1,8,16,16]{3,2,1,0:T(8,128)}, u32[]{:S(2)}) copy-start(s32[1,8,16,16]{3,2,1,0:T(8,128)} %param.9) | copy-start | bytes 24580
  5.6 7.1 %collective-permute-start.1 = (f32[8,16,1,128]{3,2,1,0:T(1,128)S(1)}, f32[8,16,1,128]{3,2,1,0:T(1,128)S(1)}, u32[]{:S(2)}, u32[]{:S(2)}) collective-permute-start(f32[8,16,1,128]{3,2,1,0:T(1,128)S(1)} %get-tuple-element.25), channel_id=1, source_target_pairs={{1,0},{2,1},{3,2},{5,4},{6,5},{7,6},{9,8},{10,9},{11,10},{13,12},{... | collective-permute-start | bytes 196616 | tf_op jit(solution)/shard_map/ppermute | solution.py:184
  6.9 7.1 %collective-permute-start.2 = (f32[8,16,1,128]{3,2,1,0:T(1,128)S(1)}, f32[8,16,1,128]{3,2,1,0:T(1,128)S(1)}, u32[]{:S(2)}, u32[]{:S(2)}) collective-permute-start(f32[8,16,1,128]{3,2,1,0:T(1,128)S(1)} %get-tuple-element.26), channel_id=1, source_target_pairs={{0,1},{1,2},{2,3},{4,5},{5,6},{6,7},{8,9},{9,10},{10,11},{12,13},{... | collective-permute-start | bytes 196616 | tf_op jit(solution)/shard_map/ppermute | solution.py:181
  14.4 1.2 %copy-start.1 = (f32[1,1,512,512]{3,2,1,0:T(8,128)S(1)}, f32[1,1,512,512]{3,2,1,0:T(8,128)}, u32[]{:S(2)}) copy-start(f32[1,1,512,512]{3,2,1,0:T(8,128)} %param.11) | copy-start | bytes 3145732
  15.2 6.1 %collective-permute-start.3 = (f32[512,128]{1,0:T(8,128)S(1)}, f32[512,128]{1,0:T(8,128)S(1)}, u32[]{:S(2)}, u32[]{:S(2)}) collective-permute-start(f32[512,128]{1,0:T(8,128)S(1)} %fusion.2.data), channel_id=1, source_target_pairs={{0,4},{4,0},{8,12},{12,8},{16,20},{20,16},{24,28},{28,24},{1,5},{5... | collective-permute-start | bytes 786440 | tf_op jit(solution)/shard_map/ppermute | solution.py:173
  18.5 9.9 %collective-permute-start.5 = (f32[256,256]{1,0:T(8,128)S(1)}, f32[256,256]{1,0:T(8,128)S(1)}, u32[]{:S(2)}, u32[]{:S(2)}) collective-permute-start(f32[256,256]{1,0:T(8,128)S(1)} %get-tuple-element.15.parent), channel_id=1, source_target_pairs={{0,8},{8,0},{4,12},{12,4},{16,24},{24,16},{20,28},{28,20},{1,9},{9... | collective-permute-start | bytes 786440 | tf_op jit(solution)/shard_map/ppermute | solution.py:173
  22.3 8.4 %collective-permute-start.4 = (f32[256,128]{1,0:T(8,128)S(1)}, f32[256,128]{1,0:T(8,128)S(1)}, u32[]{:S(2)}, u32[]{:S(2)}) collective-permute-start(f32[256,128]{1,0:T(8,128)S(1)} %get-tuple-element.14.data), channel_id=1, source_target_pairs={{0,8},{8,0},{4,12},{12,4},{16,24},{24,16},{20,28},{28,20},{1,9},{9... | collective-permute-start | bytes 393224 | tf_op jit(solution)/shard_map/ppermute | solution.py:173
  32.0 5.0 %collective-permute-start.6 = (f32[256,128]{1,0:T(8,128)S(1)}, f32[256,128]{1,0:T(8,128)S(1)}, u32[]{:S(2)}, u32[]{:S(2)}) collective-permute-start(f32[256,128]{1,0:T(8,128)S(1)} %get-tuple-element.21), channel_id=1, source_target_pairs={{0,8},{8,0},{4,12},{12,4},{16,24},{24,16},{20,28},{28,20},{1,9},{9... | collective-permute-start | bytes 393224 | tf_op jit(solution)/shard_map/ppermute | solution.py:173
where the time goes:
time: 38.3 us; the launch traced here: 37.8 us
  starting transfers between devices  11.7 us (31%)
  waiting for transfers between devices  11.6 us (30%)
  Pallas kernels  6.93 us (18%)
  other arithmetic  4.45 us (12%)
  local copies, waits for them, and re-layouts  1.54 us (4%)
  between operations  0.79 us (2%)
  matrix products  0.71 us (2%)
    ppermute x5, waiting for transfers between devices, from_partner(): return lax.ppermute(block, axis, route)  9.75 us
    pallas_call x4, Pallas kernels, local(): pl.pallas_call(kernel, out_shape=[jax.ShapeDtypeStruct(s, jnp.float32) fo...  6.93 us
    ppermute x5, starting transfers between devices, from_partner(): return lax.ppermute(block, axis, route)  5.24 us
    ppermute x1, starting transfers between devices, padded_2(): lax.ppermute(lax.slice_in_dim(block, block.shape[dim] - width, None, axis...  5.17 us
    convert_element_type x1, other arithmetic, currents(): speed = velocity.astype(jnp.float32)  1.79 us
    mul x1, other arithmetic, currents(): return (weight * elec_x, weight * elec_y, weight * elec_z)  1.4 us
    ppermute x1, starting transfers between devices, padded_2(): lax.ppermute(lax.slice_in_dim(block, 0, width, axis=dim), axis, backward)  1.29 us
    ppermute x1, waiting for transfers between devices, padded_2(): lax.ppermute(lax.slice_in_dim(block, block.shape[dim] - width, None, axis...  1.22 us
  transfers between devices with their start and end apart: 7, of which 5 were waited for; matrix products, arithmetic and copies ran while one was open for 15% of the time, Pallas kernels for 15%

commit v1 on v0

--- a/solution.py
+++ b/solution.py
@@ -11,6 +11,7 @@
 SQUARINGS = 3
 NEWTON_LIMIT = 12
 CLOSE = 0.05
+MESH = pl.DeviceIdType.MESH
 VMEM = pl.BlockSpec(memory_space=pltpu.VMEM)
 
 
@@ -173,39 +174,140 @@
     return lax.ppermute(block, axis, route)
 
 
-def padded_2(block, sides, width):
-    for axis, dim in sides:
-        count = lax.axis_size(axis)
-        forward = [(i, i + 1) for i in range(count - 1)]
-        backward = [(target, source) for source, target in forward]
-        low = lax.ppermute(
-            lax.slice_in_dim(block, block.shape[dim] - width, None, axis=dim), axis, forward
-        )
-        high = lax.ppermute(lax.slice_in_dim(block, 0, width, axis=dim), axis, backward)
-        block = jnp.concatenate([low, block, high], axis=dim)
-    return block
-
-
-def currents(velocity, field, conductivity, wall_flags):
-    sigma = conductivity * jnp.where(wall_flags == 1, WALL_RATIO, 1.0).astype(conductivity.dtype)
-    speed = velocity.astype(jnp.float32)
-    magnet = field[..., None]
-    weight = sigma[..., None]
-    elec_x = speed[1] * magnet[2] - speed[2] * magnet[1]
-    elec_y = speed[2] * magnet[0] - speed[0] * magnet[2]
-    elec_z = speed[0] * magnet[1] - speed[1] * magnet[0]
-    return (weight * elec_x, weight * elec_y, weight * elec_z)
-
-
-def divergence(flow_x, flow_y, padded_z):
-    padded_x = jnp.pad(flow_x, ((1, 1), (0, 0), (0, 0), (0, 0)))
-    padded_y = jnp.pad(flow_y, ((0, 0), (1, 1), (0, 0), (0, 0)))
-    return 0.5 * (
-        padded_x[2:]
-        - padded_x[:-2]
-        + (padded_y[:, 2:] - padded_y[:, :-2])
-        + (padded_z[:, :, 2:] - padded_z[:, :, :-2])
-    )
+def front_kernel(velocity, field, conductivity, wall_flags, solution_map, neumann, flow_x, part, ends, low_halo, high_halo, source, send_sem, receive_sem):
+    slab = lax.axis_index("slab")
+    count = lax.axis_size("slab")
+    has_low, has_high = slab > 0, slab < count - 1
+    lower = lax.max(slab - 1, 0)
+    upper = lax.min(slab + 1, count - 1)
+    barrier = pltpu.get_barrier_semaphore()
+
+    @pl.when(has_low)
+    def _():
+        pl.semaphore_signal(barrier, inc=1, device_id={"slab": lower}, device_id_type=MESH)
+
+    @pl.when(has_high)
+    def _():
+        pl.semaphore_signal(barrier, inc=1, device_id={"slab": upper}, device_id_type=MESH)
+
+    sizex, sizey, depth, snaps = part.shape
+    plane = (sizey, depth, snaps)
+    at_z = lax.broadcasted_iota(jnp.int32, plane, 1)
+    first, last = at_z == 0, at_z == depth - 1
+    none = jnp.zeros((1, depth, snaps), jnp.float32)
+    flow_x[0] = jnp.zeros(plane, jnp.float32)
+    flow_x[sizex + 1] = jnp.zeros(plane, jnp.float32)
+
+    def moved(a, steps):
+        flat = pltpu.roll(a.reshape(sizey * depth, snaps), steps, 0)
+        return flat.reshape(plane)
+
+    def current(x, carry):
+        sigma = conductivity[x] * jnp.where(wall_flags[x] == 1, WALL_RATIO, 1.0)
+        m0, m1, m2 = [
+            jnp.broadcast_to((sigma * field[d, x])[:, :, None], plane) for d in range(3)
+        ]
+        v0, v1, v2 = [velocity[d, x].astype(jnp.float32) for d in range(3)]
+        flow_x[x + 1] = v1 * m2 - v2 * m1
+        flow_y = v2 * m0 - v0 * m2
+        flow_z = v0 * m1 - v1 * m0
+        ends[0, x] = jnp.sum(jnp.where(first, flow_z, 0.0), axis=1, keepdims=True)
+        ends[1, x] = jnp.sum(jnp.where(last, flow_z, 0.0), axis=1, keepdims=True)
+        after = jnp.where(last, 0.0, moved(flow_z, sizey * depth - 1))
+        before = jnp.where(first, 0.0, moved(flow_z, 1))
+        across = jnp.concatenate([flow_y[1:], none]) - jnp.concatenate([none, flow_y[:-1]])
+        part[x] = across + (after - before)
+        return carry
+
+    lax.fori_loop(0, sizex, current, 0)
+    pl.semaphore_wait(barrier, has_low.astype(jnp.int32) + has_high.astype(jnp.int32))
+    down = pltpu.make_async_remote_copy(
+        src_ref=ends.at[0],
+        dst_ref=high_halo,
+        send_sem=send_sem.at[0],
+        recv_sem=receive_sem.at[0],
+        device_id={"slab": lower},
+        device_id_type=MESH,
+    )
+    up = pltpu.make_async_remote_copy(
+        src_ref=ends.at[1],
+        dst_ref=low_halo,
+        send_sem=send_sem.at[1],
+        recv_sem=receive_sem.at[1],
+        device_id={"slab": upper},
+        device_id_type=MESH,
+    )
+
+    @pl.when(has_low)
+    def _():
+        down.start()
+
+    @pl.when(jnp.logical_not(has_low))
+    def _():
+        low_halo[...] = jnp.zeros_like(low_halo)
+
+    @pl.when(has_high)
+    def _():
+        up.start()
+
+    @pl.when(jnp.logical_not(has_high))
+    def _():
+        high_halo[...] = jnp.zeros_like(high_halo)
+
+    def along(x, carry):
+        part[x] += flow_x[x + 2] - flow_x[x]
+        return carry
+
+    lax.fori_loop(0, sizex, along, 0)
+
+    @pl.when(has_low)
+    def _():
+        up.wait_recv()
+        down.wait_send()
+
+    @pl.when(has_high)
+    def _():
+        down.wait_recv()
+        up.wait_send()
+
+    def finish(x, carry):
+        low = jnp.broadcast_to(low_halo[x], plane)
+        high = jnp.broadcast_to(high_halo[x], plane)
+        ending = jnp.where(last, high, 0.0) - jnp.where(first, low, 0.0)
+        rows = sizey * depth
+        whole = (0.5 * (part[x] + ending)).reshape(rows, snaps)
+        source[pl.ds(pl.multiple_of(x * rows, rows), rows), :] = whole.astype(jnp.bfloat16)
+        return carry
+
+    lax.fori_loop(0, sizex, finish, 0)
+    neumann[...] = jnp.dot(solution_map[...], source[...], preferred_element_type=jnp.float32)
+
+
+def front(velocity, field, conductivity, wall_flags, solution_map):
+    _, sizex, sizey, depth, snaps = velocity.shape
+    f32 = jnp.float32
+    return pl.pallas_call(
+        front_kernel,
+        out_shape=jax.ShapeDtypeStruct((solution_map.shape[0], snaps), f32),
+        in_specs=[VMEM] * 5,
+        out_specs=VMEM,
+        scratch_shapes=[
+            pltpu.VMEM((sizex + 2, sizey, depth, snaps), f32),
+            pltpu.VMEM((sizex, sizey, depth, snaps), f32),
+            pltpu.VMEM((2, sizex, sizey, 1, snaps), f32),
+            pltpu.VMEM((sizex, sizey, 1, snaps), f32),
+            pltpu.VMEM((sizex, sizey, 1, snaps), f32),
+            pltpu.VMEM((sizex * sizey * depth, snaps), jnp.bfloat16),
+            pltpu.SemaphoreType.DMA((2,)),
+            pltpu.SemaphoreType.DMA((2,)),
+        ],
+        compiler_params=pltpu.CompilerParams(
+            collective_id=0, has_side_effects=True, vmem_limit_bytes=40 * 1024 * 1024
+        ),
+        cost_estimate=pl.CostEstimate(
+            flops=2 * solution_map.size * snaps, bytes_accessed=4 * 2**20, transcendentals=0
+        ),
+    )(velocity, field, conductivity, wall_flags, solution_map)
 
 
 def on_device(velocity, field, conductivity, wall_flags, leaf_solution, leaf_dtn):
@@ -213,16 +315,8 @@
     width = dtn_map.shape[0] // 2
     square = (width, width)
     other_map = from_partner(dtn_map, "box", 0)
-    flow_x, flow_y, flow_z = currents(velocity[0], field[0], conductivity[0], wall_flags[0])
-    solution_map = leaf_solution[0, 0]
-    sizex, sizey, depth, snaps = flow_x.shape
-    thin = (width, snaps)
-    cell_count = sizex * sizey * depth
-    padded = padded_2(flow_z, (("slab", 2),), 1)
-    source = divergence(flow_x, flow_y, padded).astype(jnp.bfloat16)
-    neumann = jnp.dot(
-        solution_map, source.reshape(cell_count, snaps), preferred_element_type=jnp.float32
-    )
+    neumann = front(velocity[0], field[0], conductivity[0], wall_flags[0], leaf_solution[0, 0])
+    thin = (width, neumann.shape[1])
     other_neumann = from_partner(neumann, "box", 0)
 
     cube = 2 * width**3

time: 38.3 us -> 37.8 us (0.987)
  Pallas kernels: 6.93 us -> 16 us
  starting transfers between devices: 11.7 us -> 3.41 us
  local copies, waits for them, and re-layouts: 1.54 us -> 5.61 us
  other arithmetic: 4.45 us -> 0.74 us
  matrix products: 0.71 us -> 0 us
  waiting for transfers between devices: 11.6 us -> 11.1 us
    pallas_call x0 -> x1, Pallas kernels: none -> 8.22 us  [front(): pl.pallas_call(front_kernel, out_shape=jax.ShapeDtypeStruct((solution_map...]
    ppermute x2 -> x0, starting transfers between devices: 6.46 us -> none  [the longest x1 5.17 us: padded_2(): lax.ppermute(lax.slice_in_dim(block, block.shape[dim] - width, None, axis...]
    unnamed x8 -> x12, local copies, waits for them, and re-layouts: 0.43 us -> 5.61 us
    convert_element_type x2 -> x0, other arithmetic: 2.3 us -> none  [the longest x1 1.79 us: currents(): speed = velocity.astype(jnp.float32)]
    ppermute x2 -> x0, waiting for transfers between devices: 1.88 us -> none  [the longest x1 1.22 us: padded_2(): lax.ppermute(lax.slice_in_dim(block, block.shape[dim] - width, None, axis...]
    ppermute x5, starting transfers between devices: 5.24 us -> 3.41 us  [from_partner(): return lax.ppermute(block, axis, route)]
    mul x2 -> x0, other arithmetic: 1.41 us -> none  [the longest x1 1.4 us: currents(): return (weight * elec_x, weight * elec_y, weight * elec_z)]
    ppermute x5, waiting for transfers between devices: 9.75 us -> 11.1 us  [from_partner(): return lax.ppermute(block, axis, route)]
  transfers between devices with their start and end apart: 7 -> 5, of which waited for: 5 -> 3; matrix products, arithmetic and copies ran while one was open for 15% -> 0% of each run, Pallas kernels for 15% -> 39%
where the time goes in v1:
time: 37.8 us; the launch traced here: 37.5 us
  Pallas kernels  16 us (42%)
  waiting for transfers between devices  11.1 us (29%)
  local copies, waits for them, and re-layouts  5.61 us (15%)
  starting transfers between devices  3.41 us (9%)
  other arithmetic  0.74 us (2%)
  between operations  0.7 us (2%)
    ppermute x5, waiting for transfers between devices, from_partner(): return lax.ppermute(block, axis, route)  11.1 us
    pallas_call x1, Pallas kernels, front(): pl.pallas_call(front_kernel, out_shape=jax.ShapeDtypeStruct((solution_map...  8.22 us
    pallas_call x4, Pallas kernels, local(): pl.pallas_call(kernel, out_shape=[jax.ShapeDtypeStruct(s, jnp.float32) fo...  7.76 us
    unnamed x12, local copies, waits for them, and re-layouts  5.61 us
    ppermute x5, starting transfers between devices, from_partner(): return lax.ppermute(block, axis, route)  3.41 us
  transfers between devices with their start and end apart: 5, of which 3 were waited for; matrix products, arithmetic and copies ran while one was open for 0% of the time, Pallas kernels for 39%

profile of v1, /device:TPU:0, one launch (start us, length us, event | category | flops | bytes accessed | tf_op | source)
XLA Modules:
  0.0 37.5 jit_solution(14297771173847950223)
XLA Ops:
  0.6 0.5 %collective-permute-start = (f32[512,512]{1,0:T(8,128)}, f32[512,512]{1,0:T(8,128)S(1)}, u32[]{:S(2)}, u32[]{:S(2)}) collective-permute-start(f32[512,512]{1,0:T(8,128)} %bitcast.11), channel_id=1, source_target_pairs={{0,4},{4,0},{8,12},{12,8},{16,20},{20,16},{24,28},{28,24},{1,5},{5... | collective-permute-start | bytes 3145736 | tf_op jit(solution)/shard_map/ppermute | solution.py:174
  1.1 0.0 copy-start
  1.2 1.6 %copy-done = bf16[1,1,512,2048]{3,2,1,0:T(8,128)(2,1)S(1)} copy-done((bf16[1,1,512,2048]{3,2,1,0:T(8,128)(2,1)S(1)}, bf16[1,1,512,2048]{3,2,1,0:T(8,128)(2,1)}, u32[]{:S(2)}) %copy-start) | copy-done | bytes 2097176
  2.7 0.0 copy-start.1
  2.7 1.4 %copy-done.1 = bf16[1,3,8,16,16,128]{5,4,3,2,1,0:T(8,128)(2,1)S(1)} copy-done((bf16[1,3,8,16,16,128]{5,4,3,2,1,0:T(8,128)(2,1)S(1)}, bf16[1,3,8,16,16,128]{5,4,3,2,1,0:T(8,128)(2,1)}, u32[]{:S(2)}) %copy-start.1) | copy-done | bytes 1572888
  4.1 0.0 copy-start.3
  4.2 0.9 %copy-done.3 = f32[1,3,8,16,16]{4,3,2,1,0:T(8,128)S(1)} copy-done((f32[1,3,8,16,16]{4,3,2,1,0:T(8,128)S(1)}, f32[1,3,8,16,16]{4,3,2,1,0:T(8,128)}, u32[]{:S(2)}) %copy-start.3) | copy-done | bytes 24600
  5.1 0.0 copy-start.4
  5.1 0.8 %copy-done.4 = f32[1,8,16,16]{3,2,1,0:T(8,128)S(1)} copy-done((f32[1,8,16,16]{3,2,1,0:T(8,128)S(1)}, f32[1,8,16,16]{3,2,1,0:T(8,128)}, u32[]{:S(2)}) %copy-start.4) | copy-done | bytes 8216
  5.9 0.0 copy-start.5
  5.9 0.8 %copy-done.5 = s32[1,8,16,16]{3,2,1,0:T(8,128)S(1)} copy-done((s32[1,8,16,16]{3,2,1,0:T(8,128)S(1)}, s32[1,8,16,16]{3,2,1,0:T(8,128)}, u32[]{:S(2)}) %copy-start.5) | copy-done | bytes 8216
  6.8 0.0 copy-start.2
  6.8 8.2 %shard_map.77.data = f32[512,128]{1,0:T(8,128)S(1)} custom-call(bf16[3,8,16,16,128]{4,3,2,1,0:T(8,128)(2,1)S(1)} %bitcast.10, f32[3,8,16,16]{3,2,1,0:T(8,128)S(1)} %bitcast.14, f32[8,16,16]{2,1,0:T(8,128)S(1)} %bitcast.15, s32[8,16,16]{2,1,0:T(8,128)S(1)} %bitcast.16, bf16[512,2048]{1,0:T(8,128)(2,1)S(1)} %bitcast.9), custom_call_target="tpu_custom_call" | custom-call | flops 268435456 | bytes 4194304 | tf_op jit(solution)/shard_map/pallas_call | solution.py:289
  15.0 0.1 collective-permute-start.1
  15.1 0.0 collective-permute-done.other
  15.1 0.0 copy-done.2
  15.1 3.6 %shard_map.78 = (f32[256,256]{1,0:T(8,128)S(1)}, f32[256,256]{1,0:T(8,128)S(1)}, f32[256,256]{1,0:T(8,128)S(1)}, f32[256,256]{1,0:T(8,128)S(1)}) custom-call(f32[512,512]{1,0:T(8,128)S(1)} %bitcast.12, f32[512,512]{1,0:T(8,128)S(1)} %collective-permute-done.other), custom_call_target="tpu_custom_call" | custom-call | flops 1006632960 | bytes 2097152 | tf_op jit(solution)/shard_map/pallas_call | solution.py:157
  18.7 0.7 %collective-permute-start.3 = (f32[256,256]{1,0:T(8,128)S(1)}, f32[256,256]{1,0:T(8,128)S(1)}, u32[]{:S(2)}, u32[]{:S(2)}) collective-permute-start(f32[256,256]{1,0:T(8,128)S(1)} %get-tuple-element.15.parent), channel_id=1, source_target_pairs={{0,8},{8,0},{4,12},{12,4},{16,24},{24,16},{20,28},{28,20},{1,9},{9... | collective-permute-start | bytes 786440 | tf_op jit(solution)/shard_map/ppermute | solution.py:174
  19.5 0.0 collective-permute-done.1.other_data
  19.5 1.0 %shard_map.79 = (f32[256,128]{1,0:T(8,128)S(1)}, f32[256,128]{1,0:T(8,128)S(1)}) custom-call(f32[512,512]{1,0:T(8,128)S(1)} %bitcast.13, f32[512,512]{1,0:T(8,128)S(1)} %collective-permute-done.other, f32[512,128]{1,0:T(8,128)S(1)} %shard_map.77.data, f32[512,128]{1,0:T(8,128)S(1)} %collective-permute-done.1.other_data, ...), custom_call_target="tpu_custom_call" | custom-call | flops 201326592 | bytes 3145728 | tf_op jit(solution)/shard_map/pallas_call | solution.py:157
  20.5 1.4 %collective-permute-start.2 = (f32[256,128]{1,0:T(8,128)S(1)}, f32[256,128]{1,0:T(8,128)S(1)}, u32[]{:S(2)}, u32[]{:S(2)}) collective-permute-start(f32[256,128]{1,0:T(8,128)S(1)} %get-tuple-element.14.data), channel_id=1, source_target_pairs={{0,8},{8,0},{4,12},{12,4},{16,24},{24,16},{20,28},{28,20},{1,9},{9... | collective-permute-start | bytes 393224 | tf_op jit(solution)/shard_map/ppermute | solution.py:174
  21.9 6.0 %collective-permute-done.3.other_parent = f32[256,256]{1,0:T(8,128)S(1)} collective-permute-done((f32[256,256]{1,0:T(8,128)S(1)}, f32[256,256]{1,0:T(8,128)S(1)}, u32[]{:S(2)}, u32[]{:S(2)}) %collective-permute-start.3) | collective-permute-done | bytes 262176 | tf_op jit(solution)/shard_map/ppermute | solution.py:174
  27.9 1.7 %shard_map.80 = (f32[256,256]{1,0:T(8,128)S(1)}, f32[256,256]{1,0:T(8,128)S(1)}) custom-call(f32[256,256]{1,0:T(8,128)S(1)} %get-tuple-element.15.parent, f32[256,256]{1,0:T(8,128)S(1)} %collective-permute-done.3.other_parent), custom_call_target="tpu_custom_call" | custom-call | flops 671088640 | bytes 524288 | tf_op jit(solution)/shard_map/pallas_call | solution.py:157
  29.7 0.6 %collective-permute-done.2.other_data = f32[256,128]{1,0:T(8,128)S(1)} collective-permute-done((f32[256,128]{1,0:T(8,128)S(1)}, f32[256,128]{1,0:T(8,128)S(1)}, u32[]{:S(2)}, u32[]{:S(2)}) %collective-permute-start.2) | collective-permute-done | bytes 131104 | tf_op jit(solution)/shard_map/ppermute | solution.py:174
  30.3 1.4 %shard_map.81 = (f32[256,128]{1,0:T(8,128)}, f32[256,128]{1,0:T(8,128)S(1)}) custom-call(f32[256,128]{1,0:T(8,128)S(1)} %get-tuple-element.14.data, f32[256,128]{1,0:T(8,128)S(1)} %collective-permute-done.2.other_data, f32[256,256]{1,0:T(8,128)S(1)} %get-tuple-element.16.schur, f32[256,256]{1,0:T(8,128)S(1)} %get-tuple-element.17.inverse, ...), custom_call_target="tpu_custom_call" | custom-call | flops 134217728 | bytes 1179648 | tf_op jit(solution)/shard_map/pallas_call | solution.py:157
  31.7 0.7 %collective-permute-start.4 = (f32[256,128]{1,0:T(8,128)S(1)}, f32[256,128]{1,0:T(8,128)S(1)}, u32[]{:S(2)}, u32[]{:S(2)}) collective-permute-start(f32[256,128]{1,0:T(8,128)S(1)} %get-tuple-element.21), channel_id=1, source_target_pairs={{0,8},{8,0},{4,12},{12,4},{16,24},{24,16},{20,28},{28,20},{1,9},{9... | collective-permute-start | bytes 393224 | tf_op jit(solution)/shard_map/ppermute | solution.py:174
  32.3 4.4 %collective-permute-done.4 = f32[256,128]{1,0:T(8,128)S(1)} collective-permute-done((f32[256,128]{1,0:T(8,128)S(1)}, f32[256,128]{1,0:T(8,128)S(1)}, u32[]{:S(2)}, u32[]{:S(2)}) %collective-permute-start.4) | collective-permute-done | bytes 131104 | tf_op jit(solution)/shard_map/ppermute | solution.py:174
  36.8 0.7 %maximum_bitcast_fusion = f32[1,1,512,128]{3,2,1,0:T(8,128)} fusion(f32[256,128]{1,0:T(8,128)S(1)} %get-tuple-element.23, f32[256,128]{1,0:T(8,128)S(1)} %get-tuple-element.22), kind=kLoop, calls=%fused_computation | loop fusion | flops 65536 | bytes 524288 | tf_op jit(solution)/shard_map/broadcast_in_dim | solution.py:349
  (1 shorter events, 0.0 us)
Async XLA Ops:
  0.6 14.4 %collective-permute-start = (f32[512,512]{1,0:T(8,128)}, f32[512,512]{1,0:T(8,128)S(1)}, u32[]{:S(2)}, u32[]{:S(2)}) collective-permute-start(f32[512,512]{1,0:T(8,128)} %bitcast.11), channel_id=1, source_target_pairs={{0,4},{4,0},{8,12},{12,8},{16,20},{20,16},{24,28},{28,24},{1,5},{5... | collective-permute-start | bytes 3145736 | tf_op jit(solution)/shard_map/ppermute | solution.py:174
  1.1 1.6 %copy-start = (bf16[1,1,512,2048]{3,2,1,0:T(8,128)(2,1)S(1)}, bf16[1,1,512,2048]{3,2,1,0:T(8,128)(2,1)}, u32[]{:S(2)}) copy-start(bf16[1,1,512,2048]{3,2,1,0:T(8,128)(2,1)} %param.10) | copy-start | bytes 6291460
  2.7 1.4 %copy-start.1 = (bf16[1,3,8,16,16,128]{5,4,3,2,1,0:T(8,128)(2,1)S(1)}, bf16[1,3,8,16,16,128]{5,4,3,2,1,0:T(8,128)(2,1)}, u32[]{:S(2)}) copy-start(bf16[1,3,8,16,16,128]{5,4,3,2,1,0:T(8,128)(2,1)} %param.6) | copy-start | bytes 4718596
  4.1 0.9 %copy-start.3 = (f32[1,3,8,16,16]{4,3,2,1,0:T(8,128)S(1)}, f32[1,3,8,16,16]{4,3,2,1,0:T(8,128)}, u32[]{:S(2)}) copy-start(f32[1,3,8,16,16]{4,3,2,1,0:T(8,128)} %param.7) | copy-start | bytes 73732
  5.1 0.8 %copy-start.4 = (f32[1,8,16,16]{3,2,1,0:T(8,128)S(1)}, f32[1,8,16,16]{3,2,1,0:T(8,128)}, u32[]{:S(2)}) copy-start(f32[1,8,16,16]{3,2,1,0:T(8,128)} %param.8) | copy-start | bytes 24580
  5.9 0.8 %copy-start.5 = (s32[1,8,16,16]{3,2,1,0:T(8,128)S(1)}, s32[1,8,16,16]{3,2,1,0:T(8,128)}, u32[]{:S(2)}) copy-start(s32[1,8,16,16]{3,2,1,0:T(8,128)} %param.9) | copy-start | bytes 24580
  6.8 8.3 %copy-start.2 = (f32[1,1,512,512]{3,2,1,0:T(8,128)S(1)}, f32[1,1,512,512]{3,2,1,0:T(8,128)}, u32[]{:S(2)}) copy-start(f32[1,1,512,512]{3,2,1,0:T(8,128)} %param.11) | copy-start | bytes 3145732
  15.0 4.5 %collective-permute-start.1 = (f32[512,128]{1,0:T(8,128)S(1)}, f32[512,128]{1,0:T(8,128)S(1)}, u32[]{:S(2)}, u32[]{:S(2)}) collective-permute-start(f32[512,128]{1,0:T(8,128)S(1)} %shard_map.77.data), channel_id=1, source_target_pairs={{0,4},{4,0},{8,12},{12,8},{16,20},{20,16},{24,28},{28,24},{1,5},{5... | collective-permute-start | bytes 786440 | tf_op jit(solution)/shard_map/ppermute | solution.py:174
  18.7 9.2 %collective-permute-start.3 = (f32[256,256]{1,0:T(8,128)S(1)}, f32[256,256]{1,0:T(8,128)S(1)}, u32[]{:S(2)}, u32[]{:S(2)}) collective-permute-start(f32[256,256]{1,0:T(8,128)S(1)} %get-tuple-element.15.parent), channel_id=1, source_target_pairs={{0,8},{8,0},{4,12},{12,4},{16,24},{24,16},{20,28},{28,20},{1,9},{9... | collective-permute-start | bytes 786440 | tf_op jit(solution)/shard_map/ppermute | solution.py:174
  20.5 9.8 %collective-permute-start.2 = (f32[256,128]{1,0:T(8,128)S(1)}, f32[256,128]{1,0:T(8,128)S(1)}, u32[]{:S(2)}, u32[]{:S(2)}) collective-permute-start(f32[256,128]{1,0:T(8,128)S(1)} %get-tuple-element.14.data), channel_id=1, source_target_pairs={{0,8},{8,0},{4,12},{12,4},{16,24},{24,16},{20,28},{28,20},{1,9},{9... | collective-permute-start | bytes 393224 | tf_op jit(solution)/shard_map/ppermute | solution.py:174
  31.7 5.1 %collective-permute-start.4 = (f32[256,128]{1,0:T(8,128)S(1)}, f32[256,128]{1,0:T(8,128)S(1)}, u32[]{:S(2)}, u32[]{:S(2)}) collective-permute-start(f32[256,128]{1,0:T(8,128)S(1)} %get-tuple-element.21), channel_id=1, source_target_pairs={{0,8},{8,0},{4,12},{12,4},{16,24},{24,16},{20,28},{28,20},{1,9},{9... | collective-permute-start | bytes 393224 | tf_op jit(solution)/shard_map/ppermute | solution.py:174

commit v2 on v1

--- a/solution.py
+++ b/solution.py
@@ -174,7 +174,13 @@
     return lax.ppermute(block, axis, route)
 
 
-def front_kernel(velocity, field, conductivity, wall_flags, solution_map, neumann, flow_x, part, ends, low_halo, high_halo, source, send_sem, receive_sem):
+def front_kernel(*refs):
+    far, (neumann,), near = refs[:5], refs[5:6], refs[6:11]
+    flow_x, part, ends, low_halo, high_halo, source, send_sem, receive_sem, load_sem = refs[11:]
+    velocity, field, conductivity, wall_flags, solution_map = near
+    loads = [pltpu.make_async_copy(far[i], near[i], load_sem.at[i]) for i in range(5)]
+    for i in (1, 2, 3, 0, 4):
+        loads[i].start()
     slab = lax.axis_index("slab")
     count = lax.axis_size("slab")
     has_low, has_high = slab > 0, slab < count - 1
@@ -219,6 +225,8 @@
         part[x] = across + (after - before)
         return carry
 
+    for i in range(4):
+        loads[i].wait()
     lax.fori_loop(0, sizex, current, 0)
     pl.semaphore_wait(barrier, has_low.astype(jnp.int32) + has_high.astype(jnp.int32))
     down = pltpu.make_async_remote_copy(
@@ -280,18 +288,21 @@
         return carry
 
     lax.fori_loop(0, sizex, finish, 0)
+    loads[4].wait()
     neumann[...] = jnp.dot(solution_map[...], source[...], preferred_element_type=jnp.float32)
 
 
 def front(velocity, field, conductivity, wall_flags, solution_map):
+    arrays = (velocity, field, conductivity, wall_flags, solution_map)
     _, sizex, sizey, depth, snaps = velocity.shape
     f32 = jnp.float32
     return pl.pallas_call(
         front_kernel,
         out_shape=jax.ShapeDtypeStruct((solution_map.shape[0], snaps), f32),
-        in_specs=[VMEM] * 5,
+        in_specs=[pl.BlockSpec(memory_space=pltpu.MemorySpace.HBM)] * 5,
         out_specs=VMEM,
-        scratch_shapes=[
+        scratch_shapes=[pltpu.VMEM(a.shape, a.dtype) for a in arrays]
+        + [
             pltpu.VMEM((sizex + 2, sizey, depth, snaps), f32),
             pltpu.VMEM((sizex, sizey, depth, snaps), f32),
             pltpu.VMEM((2, sizex, sizey, 1, snaps), f32),
@@ -300,6 +311,7 @@
             pltpu.VMEM((sizex * sizey * depth, snaps), jnp.bfloat16),
             pltpu.SemaphoreType.DMA((2,)),
             pltpu.SemaphoreType.DMA((2,)),
+            pltpu.SemaphoreType.DMA((5,)),
         ],
         compiler_params=pltpu.CompilerParams(
             collective_id=0, has_side_effects=True, vmem_limit_bytes=40 * 1024 * 1024
@@ -307,7 +319,7 @@
         cost_estimate=pl.CostEstimate(
             flops=2 * solution_map.size * snaps, bytes_accessed=4 * 2**20, transcendentals=0
         ),
-    )(velocity, field, conductivity, wall_flags, solution_map)
+    )(*arrays)
 
 
 def on_device(velocity, field, conductivity, wall_flags, leaf_solution, leaf_dtn):
@@ -315,14 +327,14 @@
     width = dtn_map.shape[0] // 2
     square = (width, width)
     other_map = from_partner(dtn_map, "box", 0)
+    cube = 2 * width**3
+    schur, inverse, parent, outward = local(
+        map_kernel, [square] * 4, 30 * cube, dtn_map, other_map
+    )
+    velocity, parent = lax.optimization_barrier((velocity, parent))
     neumann = front(velocity[0], field[0], conductivity[0], wall_flags[0], leaf_solution[0, 0])
     thin = (width, neumann.shape[1])
     other_neumann = from_partner(neumann, "box", 0)
-
-    cube = 2 * width**3
-    schur, inverse, parent, outward = local(
-        map_kernel, [square] * 4, 30 * cube, dtn_map, other_map
-    )
     other_parent = from_partner(parent, "box", 1)
     schur_two, inverse_two = local(
         second_map_kernel, [square] * 2, 20 * cube, parent, other_parent

time: 37.8 us -> 37.9 us (level)
  local copies, waits for them, and re-layouts: 5.61 us -> 3 us
  starting transfers between devices: 3.41 us -> 5.85 us
    unnamed x12 -> x14, local copies, waits for them, and re-layouts: 5.61 us -> 3 us
    ppermute x5, starting transfers between devices: 3.41 us -> 5.85 us  [from_partner(): return lax.ppermute(block, axis, route)]
    pallas_call x1, Pallas kernels: 8.22 us -> 9.22 us  [front(): pl.pallas_call(front_kernel, out_shape=jax.ShapeDtypeStruct((solution_map...]
    pallas_call x4, Pallas kernels: 7.76 us -> 6.93 us  [local(): pl.pallas_call(kernel, out_shape=[jax.ShapeDtypeStruct(s, jnp.float32) fo...]
  transfers between devices with their start and end apart: 5 -> 5, of which waited for: 3 -> 4; matrix products, arithmetic and copies ran while one was open for 0% -> 0% of each run, Pallas kernels for 39% -> 7%
where the time goes in v2:
time: 37.9 us
  Pallas kernels  16.2 us (43%)
  waiting for transfers between devices  11.4 us (30%)
  starting transfers between devices  5.85 us (15%)
  local copies, waits for them, and re-layouts  3 us (8%)
  other arithmetic  0.74 us (2%)
  between operations  0.73 us (2%)
    ppermute x5, waiting for transfers between devices, from_partner(): return lax.ppermute(block, axis, route)  11.4 us
    pallas_call x1, Pallas kernels, front(): pl.pallas_call(front_kernel, out_shape=jax.ShapeDtypeStruct((solution_map...  9.22 us
    pallas_call x4, Pallas kernels, local(): pl.pallas_call(kernel, out_shape=[jax.ShapeDtypeStruct(s, jnp.float32) fo...  6.93 us
    ppermute x5, starting transfers between devices, from_partner(): return lax.ppermute(block, axis, route)  5.85 us
    unnamed x14, local copies, waits for them, and re-layouts  3 us
  transfers between devices with their start and end apart: 5, of which 4 were waited for; matrix products, arithmetic and copies ran while one was open for 0% of the time, Pallas kernels for 7%

profile of v2, /device:TPU:0, one launch (start us, length us, event | category | flops | bytes accessed | tf_op | source)
XLA Modules:
  0.0 37.9 jit_solution(2297875004775770050)
XLA Ops:
  0.6 0.0 copy-start.1
  0.6 0.0 copy-start
  0.6 0.5 %collective-permute-start = (f32[512,512]{1,0:T(8,128)}, f32[512,512]{1,0:T(8,128)S(1)}, u32[]{:S(2)}, u32[]{:S(2)}) collective-permute-start(f32[512,512]{1,0:T(8,128)} %bitcast.11), channel_id=1, source_target_pairs={{0,4},{4,0},{8,12},{12,8},{16,20},{20,16},{24,28},{28,24},{1,5},{5... | collective-permute-start | bytes 3145736 | tf_op jit(solution)/shard_map/ppermute | solution.py:174
  1.2 2.5 %collective-permute-done.other = f32[512,512]{1,0:T(8,128)S(1)} collective-permute-done((f32[512,512]{1,0:T(8,128)}, f32[512,512]{1,0:T(8,128)S(1)}, u32[]{:S(2)}, u32[]{:S(2)}) %collective-permute-start) | collective-permute-done | bytes 1048608 | tf_op jit(solution)/shard_map/ppermute | solution.py:174
  3.7 0.0 copy-start.2
  3.7 1.2 %copy-done.2 = f32[1,1,512,512]{3,2,1,0:T(8,128)S(1)} copy-done((f32[1,1,512,512]{3,2,1,0:T(8,128)S(1)}, f32[1,1,512,512]{3,2,1,0:T(8,128)}, u32[]{:S(2)}) %copy-start.2) | copy-done | bytes 1048600
  4.9 0.0 copy-start.5
  4.9 2.8 %shard_map.77 = (f32[256,256]{1,0:T(8,128)S(1)}, f32[256,256]{1,0:T(8,128)S(1)}, f32[256,256]{1,0:T(8,128)S(1)}, f32[256,256]{1,0:T(8,128)S(1)}) custom-call(f32[512,512]{1,0:T(8,128)S(1)} %bitcast.12, f32[512,512]{1,0:T(8,128)S(1)} %collective-permute-done.other), custom_call_target="tpu_custom_call" | custom-call | flops 1006632960 | bytes 2097152 | tf_op jit(solution)/shard_map/pallas_call | solution.py:157
  7.7 0.0 copy-done.1
  7.7 0.0 copy-done
  7.7 0.0 copy-done.5
  7.7 0.0 copy-start.4
  7.8 0.9 %copy-done.4 = f32[1,3,8,16,16]{4,3,2,1,0:T(8,128)S(1)} copy-done((f32[1,3,8,16,16]{4,3,2,1,0:T(8,128)S(1)}, f32[1,3,8,16,16]{4,3,2,1,0:T(8,128)}, u32[]{:S(2)}) %copy-start.4) | copy-done | bytes 24600
  8.7 0.0 copy-start.6
  8.7 0.8 %copy-done.6 = s32[1,8,16,16]{3,2,1,0:T(8,128)S(1)} copy-done((s32[1,8,16,16]{3,2,1,0:T(8,128)S(1)}, s32[1,8,16,16]{3,2,1,0:T(8,128)}, u32[]{:S(2)}) %copy-start.6) | copy-done | bytes 8216
  9.5 0.0 copy-start.3
  9.5 9.2 %shard_map.78.data = f32[512,128]{1,0:T(8,128)S(1)} custom-call(bf16[3,8,16,16,128]{4,3,2,1,0:T(8,128)(2,1)S(1)} %bitcast.10, f32[3,8,16,16]{3,2,1,0:T(8,128)S(1)} %bitcast.14, f32[8,16,16]{2,1,0:T(8,128)S(1)} %bitcast.15, s32[8,16,16]{2,1,0:T(8,128)S(1)} %bitcast.16, bf16[512,2048]{1,0:T(8,128)(2,1)S(1)} %bitcast.9), custom_call_target="tpu_custom_call" | custom-call | flops 268435456 | bytes 4194304 | tf_op jit(solution)/shard_map/pallas_call | solution.py:299
  18.7 0.1 collective-permute-start.1
  18.8 2.0 %collective-permute-start.3 = (f32[256,256]{1,0:T(8,128)S(1)}, f32[256,256]{1,0:T(8,128)S(1)}, u32[]{:S(2)}, u32[]{:S(2)}) collective-permute-start(f32[256,256]{1,0:T(8,128)S(1)} %get-tuple-element.19.parent), channel_id=1, source_target_pairs={{0,8},{8,0},{4,12},{12,4},{16,24},{24,16},{20,28},{28,20},{1,9},{9... | collective-permute-start | bytes 786440 | tf_op jit(solution)/shard_map/ppermute | solution.py:174
  20.8 0.0 collective-permute-done.1.other_data
  20.8 0.0 copy-done.3
  20.8 1.0 %shard_map.79 = (f32[256,128]{1,0:T(8,128)S(1)}, f32[256,128]{1,0:T(8,128)S(1)}) custom-call(f32[512,512]{1,0:T(8,128)S(1)} %bitcast.13, f32[512,512]{1,0:T(8,128)S(1)} %collective-permute-done.other, f32[512,128]{1,0:T(8,128)S(1)} %shard_map.78.data, f32[512,128]{1,0:T(8,128)S(1)} %collective-permute-done.1.other_data, ...), custom_call_target="tpu_custom_call" | custom-call | flops 201326592 | bytes 3145728 | tf_op jit(solution)/shard_map/pallas_call | solution.py:157
  21.8 1.5 %collective-permute-start.2 = (f32[256,128]{1,0:T(8,128)S(1)}, f32[256,128]{1,0:T(8,128)S(1)}, u32[]{:S(2)}, u32[]{:S(2)}) collective-permute-start(f32[256,128]{1,0:T(8,128)S(1)} %get-tuple-element.18.data), channel_id=1, source_target_pairs={{0,8},{8,0},{4,12},{12,4},{16,24},{24,16},{20,28},{28,20},{1,9},{9... | collective-permute-start | bytes 393224 | tf_op jit(solution)/shard_map/ppermute | solution.py:174
  23.3 4.6 %collective-permute-done.3.other_parent = f32[256,256]{1,0:T(8,128)S(1)} collective-permute-done((f32[256,256]{1,0:T(8,128)S(1)}, f32[256,256]{1,0:T(8,128)S(1)}, u32[]{:S(2)}, u32[]{:S(2)}) %collective-permute-start.3) | collective-permute-done | bytes 262176 | tf_op jit(solution)/shard_map/ppermute | solution.py:174
  28.0 1.7 %shard_map.80 = (f32[256,256]{1,0:T(8,128)S(1)}, f32[256,256]{1,0:T(8,128)S(1)}) custom-call(f32[256,256]{1,0:T(8,128)S(1)} %get-tuple-element.19.parent, f32[256,256]{1,0:T(8,128)S(1)} %collective-permute-done.3.other_parent), custom_call_target="tpu_custom_call" | custom-call | flops 671088640 | bytes 524288 | tf_op jit(solution)/shard_map/pallas_call | solution.py:157
  29.7 0.8 %collective-permute-done.2.other_data = f32[256,128]{1,0:T(8,128)S(1)} collective-permute-done((f32[256,128]{1,0:T(8,128)S(1)}, f32[256,128]{1,0:T(8,128)S(1)}, u32[]{:S(2)}, u32[]{:S(2)}) %collective-permute-start.2) | collective-permute-done | bytes 131104 | tf_op jit(solution)/shard_map/ppermute | solution.py:174
  30.5 1.4 %shard_map.81 = (f32[256,128]{1,0:T(8,128)}, f32[256,128]{1,0:T(8,128)S(1)}) custom-call(f32[256,128]{1,0:T(8,128)S(1)} %get-tuple-element.18.data, f32[256,128]{1,0:T(8,128)S(1)} %collective-permute-done.2.other_data, f32[256,256]{1,0:T(8,128)S(1)} %get-tuple-element.20.schur, f32[256,256]{1,0:T(8,128)S(1)} %get-tuple-element.21.inverse, ...), custom_call_target="tpu_custom_call" | custom-call | flops 134217728 | bytes 1179648 | tf_op jit(solution)/shard_map/pallas_call | solution.py:157
  31.9 1.8 %collective-permute-start.4 = (f32[256,128]{1,0:T(8,128)S(1)}, f32[256,128]{1,0:T(8,128)S(1)}, u32[]{:S(2)}, u32[]{:S(2)}) collective-permute-start(f32[256,128]{1,0:T(8,128)S(1)} %get-tuple-element.25), channel_id=1, source_target_pairs={{0,8},{8,0},{4,12},{12,4},{16,24},{24,16},{20,28},{28,20},{1,9},{9... | collective-permute-start | bytes 393224 | tf_op jit(solution)/shard_map/ppermute | solution.py:174
  33.7 3.5 %collective-permute-done.4 = f32[256,128]{1,0:T(8,128)S(1)} collective-permute-done((f32[256,128]{1,0:T(8,128)S(1)}, f32[256,128]{1,0:T(8,128)S(1)}, u32[]{:S(2)}, u32[]{:S(2)}) %collective-permute-start.4) | collective-permute-done | bytes 131104 | tf_op jit(solution)/shard_map/ppermute | solution.py:174
  37.2 0.7 %maximum_bitcast_fusion = f32[1,1,512,128]{3,2,1,0:T(8,128)} fusion(f32[256,128]{1,0:T(8,128)S(1)} %get-tuple-element.27, f32[256,128]{1,0:T(8,128)S(1)} %get-tuple-element.26), kind=kLoop, calls=%fused_computation | loop fusion | flops 65536 | bytes 524288 | tf_op jit(solution)/shard_map/broadcast_in_dim | solution.py:361
  (1 shorter events, 0.0 us)
Async XLA Ops:
  0.6 7.1 %copy-start.1 = (bf16[1,3,8,16,16,128]{5,4,3,2,1,0:T(8,128)(2,1)S(1)}, bf16[1,3,8,16,16,128]{5,4,3,2,1,0:T(8,128)(2,1)}, u32[]{:S(2)}) copy-start(bf16[1,3,8,16,16,128]{5,4,3,2,1,0:T(8,128)(2,1)} %param.6) | copy-start | bytes 4718596
  0.6 7.1 %copy-start = (bf16[1,1,512,2048]{3,2,1,0:T(8,128)(2,1)S(1)}, bf16[1,1,512,2048]{3,2,1,0:T(8,128)(2,1)}, u32[]{:S(2)}) copy-start(bf16[1,1,512,2048]{3,2,1,0:T(8,128)(2,1)} %param.10) | copy-start | bytes 6291460
  0.6 3.0 %collective-permute-start = (f32[512,512]{1,0:T(8,128)}, f32[512,512]{1,0:T(8,128)S(1)}, u32[]{:S(2)}, u32[]{:S(2)}) collective-permute-start(f32[512,512]{1,0:T(8,128)} %bitcast.11), channel_id=1, source_target_pairs={{0,4},{4,0},{8,12},{12,8},{16,20},{20,16},{24,28},{28,24},{1,5},{5... | collective-permute-start | bytes 3145736 | tf_op jit(solution)/shard_map/ppermute | solution.py:174
  3.7 1.2 %copy-start.2 = (f32[1,1,512,512]{3,2,1,0:T(8,128)S(1)}, f32[1,1,512,512]{3,2,1,0:T(8,128)}, u32[]{:S(2)}) copy-start(f32[1,1,512,512]{3,2,1,0:T(8,128)} %param.11) | copy-start | bytes 3145732
  4.9 2.8 %copy-start.5 = (f32[1,8,16,16]{3,2,1,0:T(8,128)S(1)}, f32[1,8,16,16]{3,2,1,0:T(8,128)}, u32[]{:S(2)}) copy-start(f32[1,8,16,16]{3,2,1,0:T(8,128)} %param.8) | copy-start | bytes 24580
  7.7 0.9 %copy-start.4 = (f32[1,3,8,16,16]{4,3,2,1,0:T(8,128)S(1)}, f32[1,3,8,16,16]{4,3,2,1,0:T(8,128)}, u32[]{:S(2)}) copy-start(f32[1,3,8,16,16]{4,3,2,1,0:T(8,128)} %param.7) | copy-start | bytes 73732
  8.7 0.8 %copy-start.6 = (s32[1,8,16,16]{3,2,1,0:T(8,128)S(1)}, s32[1,8,16,16]{3,2,1,0:T(8,128)}, u32[]{:S(2)}) copy-start(s32[1,8,16,16]{3,2,1,0:T(8,128)} %param.9) | copy-start | bytes 24580
  9.5 11.3 %copy-start.3 = (f32[1,1,512,512]{3,2,1,0:T(8,128)S(1)}, f32[1,1,512,512]{3,2,1,0:T(8,128)}, u32[]{:S(2)}) copy-start(f32[1,1,512,512]{3,2,1,0:T(8,128)} %param.11) | copy-start | bytes 3145732
  18.7 2.1 %collective-permute-start.1 = (f32[512,128]{1,0:T(8,128)S(1)}, f32[512,128]{1,0:T(8,128)S(1)}, u32[]{:S(2)}, u32[]{:S(2)}) collective-permute-start(f32[512,128]{1,0:T(8,128)S(1)} %shard_map.78.data), channel_id=1, source_target_pairs={{0,4},{4,0},{8,12},{12,8},{16,20},{20,16},{24,28},{28,24},{1,5},{5... | collective-permute-start | bytes 786440 | tf_op jit(solution)/shard_map/ppermute | solution.py:174
  18.8 9.2 %collective-permute-start.3 = (f32[256,256]{1,0:T(8,128)S(1)}, f32[256,256]{1,0:T(8,128)S(1)}, u32[]{:S(2)}, u32[]{:S(2)}) collective-permute-start(f32[256,256]{1,0:T(8,128)S(1)} %get-tuple-element.19.parent), channel_id=1, source_target_pairs={{0,8},{8,0},{4,12},{12,4},{16,24},{24,16},{20,28},{28,20},{1,9},{9... | collective-permute-start | bytes 786440 | tf_op jit(solution)/shard_map/ppermute | solution.py:174
  21.8 8.7 %collective-permute-start.2 = (f32[256,128]{1,0:T(8,128)S(1)}, f32[256,128]{1,0:T(8,128)S(1)}, u32[]{:S(2)}, u32[]{:S(2)}) collective-permute-start(f32[256,128]{1,0:T(8,128)S(1)} %get-tuple-element.18.data), channel_id=1, source_target_pairs={{0,8},{8,0},{4,12},{12,4},{16,24},{24,16},{20,28},{28,20},{1,9},{9... | collective-permute-start | bytes 393224 | tf_op jit(solution)/shard_map/ppermute | solution.py:174
  31.9 5.3 %collective-permute-start.4 = (f32[256,128]{1,0:T(8,128)S(1)}, f32[256,128]{1,0:T(8,128)S(1)}, u32[]{:S(2)}, u32[]{:S(2)}) collective-permute-start(f32[256,128]{1,0:T(8,128)S(1)} %get-tuple-element.25), channel_id=1, source_target_pairs={{0,8},{8,0},{4,12},{12,4},{16,24},{24,16},{20,28},{28,20},{1,9},{9... | collective-permute-start | bytes 393224 | tf_op jit(solution)/shard_map/ppermute | solution.py:174

commit v3 on v2

--- a/solution.py
+++ b/solution.py
@@ -175,8 +175,9 @@
 
 
 def front_kernel(*refs):
-    far, (neumann,), near = refs[:5], refs[5:6], refs[6:11]
-    flow_x, part, ends, low_halo, high_halo, source, send_sem, receive_sem, load_sem = refs[11:]
+    far, near = refs[:5], refs[8:13]
+    parent, neumann, other_parent = refs[5:8]
+    flow_x, part, ends, low_halo, high_halo, source, send_sem, receive_sem, load_sem = refs[13:]
     velocity, field, conductivity, wall_flags, solution_map = near
     loads = [pltpu.make_async_copy(far[i], near[i], load_sem.at[i]) for i in range(5)]
     for i in (1, 2, 3, 0, 4):
@@ -186,7 +187,10 @@
     has_low, has_high = slab > 0, slab < count - 1
     lower = lax.max(slab - 1, 0)
     upper = lax.min(slab + 1, count - 1)
+    box = lax.axis_index("box")
+    across_box = box + 2 - 4 * lax.rem(lax.div(box, 2), 2)
     barrier = pltpu.get_barrier_semaphore()
+    pl.semaphore_signal(barrier, inc=1, device_id={"box": across_box}, device_id_type=MESH)
 
     @pl.when(has_low)
     def _():
@@ -228,7 +232,7 @@
     for i in range(4):
         loads[i].wait()
     lax.fori_loop(0, sizex, current, 0)
-    pl.semaphore_wait(barrier, has_low.astype(jnp.int32) + has_high.astype(jnp.int32))
+    pl.semaphore_wait(barrier, 1 + has_low.astype(jnp.int32) + has_high.astype(jnp.int32))
     down = pltpu.make_async_remote_copy(
         src_ref=ends.at[0],
         dst_ref=high_halo,
@@ -246,6 +250,15 @@
         device_id_type=MESH,
     )
 
+    swap = pltpu.make_async_remote_copy(
+        src_ref=parent,
+        dst_ref=other_parent,
+        send_sem=send_sem.at[2],
+        recv_sem=receive_sem.at[2],
+        device_id={"box": across_box},
+        device_id_type=MESH,
+    )
+
     @pl.when(has_low)
     def _():
         down.start()
@@ -261,6 +274,8 @@
     @pl.when(jnp.logical_not(has_high))
     def _():
         high_halo[...] = jnp.zeros_like(high_halo)
+
+    swap.start()
 
     def along(x, carry):
         part[x] += flow_x[x + 2] - flow_x[x]
@@ -290,17 +305,21 @@
     lax.fori_loop(0, sizex, finish, 0)
     loads[4].wait()
     neumann[...] = jnp.dot(solution_map[...], source[...], preferred_element_type=jnp.float32)
-
-
-def front(velocity, field, conductivity, wall_flags, solution_map):
+    swap.wait()
+
+
+def front(velocity, field, conductivity, wall_flags, solution_map, parent):
     arrays = (velocity, field, conductivity, wall_flags, solution_map)
     _, sizex, sizey, depth, snaps = velocity.shape
     f32 = jnp.float32
     return pl.pallas_call(
         front_kernel,
-        out_shape=jax.ShapeDtypeStruct((solution_map.shape[0], snaps), f32),
-        in_specs=[pl.BlockSpec(memory_space=pltpu.MemorySpace.HBM)] * 5,
-        out_specs=VMEM,
+        out_shape=[
+            jax.ShapeDtypeStruct((solution_map.shape[0], snaps), f32),
+            jax.ShapeDtypeStruct(parent.shape, f32),
+        ],
+        in_specs=[pl.BlockSpec(memory_space=pltpu.MemorySpace.HBM)] * 5 + [VMEM],
+        out_specs=[VMEM] * 2,
         scratch_shapes=[pltpu.VMEM(a.shape, a.dtype) for a in arrays]
         + [
             pltpu.VMEM((sizex + 2, sizey, depth, snaps), f32),
@@ -309,8 +328,8 @@
             pltpu.VMEM((sizex, sizey, 1, snaps), f32),
             pltpu.VMEM((sizex, sizey, 1, snaps), f32),
             pltpu.VMEM((sizex * sizey * depth, snaps), jnp.bfloat16),
-            pltpu.SemaphoreType.DMA((2,)),
-            pltpu.SemaphoreType.DMA((2,)),
+            pltpu.SemaphoreType.DMA((3,)),
+            pltpu.SemaphoreType.DMA((3,)),
             pltpu.SemaphoreType.DMA((5,)),
         ],
         compiler_params=pltpu.CompilerParams(
@@ -319,7 +338,7 @@
         cost_estimate=pl.CostEstimate(
             flops=2 * solution_map.size * snaps, bytes_accessed=4 * 2**20, transcendentals=0
         ),
-    )(*arrays)
+    )(*arrays, parent)
 
 
 def on_device(velocity, field, conductivity, wall_flags, leaf_solution, leaf_dtn):
@@ -331,11 +350,11 @@
     schur, inverse, parent, outward = local(
         map_kernel, [square] * 4, 30 * cube, dtn_map, other_map
     )
-    velocity, parent = lax.optimization_barrier((velocity, parent))
-    neumann = front(velocity[0], field[0], conductivity[0], wall_flags[0], leaf_solution[0, 0])
+    neumann, other_parent = front(
+        velocity[0], field[0], conductivity[0], wall_flags[0], leaf_solution[0, 0], parent
+    )
     thin = (width, neumann.shape[1])
     other_neumann = from_partner(neumann, "box", 0)
-    other_parent = from_partner(parent, "box", 1)
     schur_two, inverse_two = local(
         second_map_kernel, [square] * 2, 20 * cube, parent, other_parent
     )

time: 37.9 us -> 37.6 us (level); the launches traced: 37.9 us -> 36.9 us
  starting transfers between devices: 5.85 us -> 2.28 us
  Pallas kernels: 16.2 us -> 19 us
    ppermute x5 -> x4, starting transfers between devices: 5.85 us -> 2.28 us  [from_partner(): return lax.ppermute(block, axis, route)]
    pallas_call x1, Pallas kernels: 9.22 us -> 11.3 us  [front(): pl.pallas_call(front_kernel, out_shape=[jax.ShapeDtypeStruct((solution_ma...]
    pallas_call x4, Pallas kernels: 6.93 us -> 7.74 us  [local(): pl.pallas_call(kernel, out_shape=[jax.ShapeDtypeStruct(s, jnp.float32) fo...]
    ppermute x5 -> x4, waiting for transfers between devices: 11.4 us -> 11.2 us  [from_partner(): return lax.ppermute(block, axis, route)]
  transfers between devices with their start and end apart: 5 -> 4, of which waited for: 4 -> 4; matrix products, arithmetic and copies ran while one was open for 0% -> 0% of each run, Pallas kernels for 7% -> 5%
where the time goes in v3:
time: 37.6 us; the launch traced here: 36.9 us
  Pallas kernels  19 us (51%)
  waiting for transfers between devices  11.2 us (30%)
  local copies, waits for them, and re-layouts  3 us (8%)
  starting transfers between devices  2.28 us (6%)
  other arithmetic  0.74 us (2%)
  between operations  0.73 us (2%)
    pallas_call x1, Pallas kernels, front(): pl.pallas_call(front_kernel, out_shape=[jax.ShapeDtypeStruct((solution_ma...  11.3 us
    ppermute x4, waiting for transfers between devices, from_partner(): return lax.ppermute(block, axis, route)  11.2 us
    pallas_call x4, Pallas kernels, local(): pl.pallas_call(kernel, out_shape=[jax.ShapeDtypeStruct(s, jnp.float32) fo...  7.74 us
    unnamed x14, local copies, waits for them, and re-layouts  3 us
    ppermute x4, starting transfers between devices, from_partner(): return lax.ppermute(block, axis, route)  2.28 us
  transfers between devices with their start and end apart: 4, of which 4 were waited for; matrix products, arithmetic and copies ran while one was open for 0% of the time, Pallas kernels for 5%

profile of v3, /device:TPU:0, one launch (start us, length us, event | category | flops | bytes accessed | tf_op | source)
XLA Modules:
  0.0 36.9 jit_solution(6000458806712385796)
XLA Ops:
  0.6 0.0 copy-start.1
  0.6 0.0 copy-start
  0.6 0.5 %collective-permute-start = (f32[512,512]{1,0:T(8,128)}, f32[512,512]{1,0:T(8,128)S(1)}, u32[]{:S(2)}, u32[]{:S(2)}) collective-permute-start(f32[512,512]{1,0:T(8,128)} %bitcast.11), channel_id=1, source_target_pairs={{0,4},{4,0},{8,12},{12,8},{16,20},{20,16},{24,28},{28,24},{1,5},{5... | collective-permute-start | bytes 3145736 | tf_op jit(solution)/shard_map/ppermute | solution.py:174
  1.2 2.5 %collective-permute-done.other = f32[512,512]{1,0:T(8,128)S(1)} collective-permute-done((f32[512,512]{1,0:T(8,128)}, f32[512,512]{1,0:T(8,128)S(1)}, u32[]{:S(2)}, u32[]{:S(2)}) %collective-permute-start) | collective-permute-done | bytes 1048608 | tf_op jit(solution)/shard_map/ppermute | solution.py:174
  3.7 0.0 copy-start.2
  3.7 1.2 %copy-done.2 = f32[1,1,512,512]{3,2,1,0:T(8,128)S(1)} copy-done((f32[1,1,512,512]{3,2,1,0:T(8,128)S(1)}, f32[1,1,512,512]{3,2,1,0:T(8,128)}, u32[]{:S(2)}) %copy-start.2) | copy-done | bytes 1048600
  4.9 0.0 copy-start.5
  4.9 3.6 %shard_map.77 = (f32[256,256]{1,0:T(8,128)S(1)}, f32[256,256]{1,0:T(8,128)S(1)}, f32[256,256]{1,0:T(8,128)S(1)}, f32[256,256]{1,0:T(8,128)S(1)}) custom-call(f32[512,512]{1,0:T(8,128)S(1)} %bitcast.12, f32[512,512]{1,0:T(8,128)S(1)} %collective-permute-done.other), custom_call_target="tpu_custom_call" | custom-call | flops 1006632960 | bytes 2097152 | tf_op jit(solution)/shard_map/pallas_call | solution.py:157
  8.5 0.0 copy-done.1
  8.5 0.0 copy-done
  8.6 0.0 copy-done.5
  8.6 0.0 copy-start.4
  8.6 0.9 %copy-done.4 = f32[1,3,8,16,16]{4,3,2,1,0:T(8,128)S(1)} copy-done((f32[1,3,8,16,16]{4,3,2,1,0:T(8,128)S(1)}, f32[1,3,8,16,16]{4,3,2,1,0:T(8,128)}, u32[]{:S(2)}) %copy-start.4) | copy-done | bytes 24600
  9.5 0.0 copy-start.6
  9.5 0.8 %copy-done.6 = s32[1,8,16,16]{3,2,1,0:T(8,128)S(1)} copy-done((s32[1,8,16,16]{3,2,1,0:T(8,128)S(1)}, s32[1,8,16,16]{3,2,1,0:T(8,128)}, u32[]{:S(2)}) %copy-start.6) | copy-done | bytes 8216
  10.3 0.0 copy-start.3
  10.3 11.3 %shard_map.78 = (f32[512,128]{1,0:T(8,128)S(1)}, f32[256,256]{1,0:T(8,128)S(1)}) custom-call(bf16[3,8,16,16,128]{4,3,2,1,0:T(8,128)(2,1)S(1)} %bitcast.10, f32[3,8,16,16]{3,2,1,0:T(8,128)S(1)} %bitcast.14, f32[8,16,16]{2,1,0:T(8,128)S(1)} %bitcast.15, s32[8,16,16]{2,1,0:T(8,128)S(1)} %bitcast.16, bf16[512,2048]{1,0:T(8,128)(2,1)S(1)} %bitcast.9, ...), custom_call_target="tpu_custom_call" | custom-call | flops 268435456 | bytes 4194304 | tf_op jit(solution)/shard_map/pallas_call | solution.py:315
  21.6 0.1 collective-permute-start.1
  21.7 1.5 %collective-permute-done.1.other_data = f32[512,128]{1,0:T(8,128)S(1)} collective-permute-done((f32[512,128]{1,0:T(8,128)S(1)}, f32[512,128]{1,0:T(8,128)S(1)}, u32[]{:S(2)}, u32[]{:S(2)}) %collective-permute-start.1) | collective-permute-done | bytes 262176 | tf_op jit(solution)/shard_map/ppermute | solution.py:174
  23.2 0.0 copy-done.3
  23.2 1.0 %shard_map.79 = (f32[256,128]{1,0:T(8,128)S(1)}, f32[256,128]{1,0:T(8,128)S(1)}) custom-call(f32[512,512]{1,0:T(8,128)S(1)} %bitcast.13, f32[512,512]{1,0:T(8,128)S(1)} %collective-permute-done.other, f32[512,128]{1,0:T(8,128)S(1)} %get-tuple-element.15.data, f32[512,128]{1,0:T(8,128)S(1)} %collective-permute-done.1.other_data, ...), custom_call_target="tpu_custom_call" | custom-call | flops 201326592 | bytes 3145728 | tf_op jit(solution)/shard_map/pallas_call | solution.py:157
  24.2 0.9 %collective-permute-start.2 = (f32[256,128]{1,0:T(8,128)S(1)}, f32[256,128]{1,0:T(8,128)S(1)}, u32[]{:S(2)}, u32[]{:S(2)}) collective-permute-start(f32[256,128]{1,0:T(8,128)S(1)} %get-tuple-element.18.data), channel_id=1, source_target_pairs={{0,8},{8,0},{4,12},{12,4},{16,24},{24,16},{20,28},{28,20},{1,9},{9... | collective-permute-start | bytes 393224 | tf_op jit(solution)/shard_map/ppermute | solution.py:174
  25.1 1.7 %shard_map.80 = (f32[256,256]{1,0:T(8,128)S(1)}, f32[256,256]{1,0:T(8,128)S(1)}) custom-call(f32[256,256]{1,0:T(8,128)S(1)} %get-tuple-element.14.refs_5_.parent, f32[256,256]{1,0:T(8,128)S(1)} %get-tuple-element.19.other_parent), custom_call_target="tpu_custom_call" | custom-call | flops 671088640 | bytes 524288 | tf_op jit(solution)/shard_map/pallas_call | solution.py:157
  26.9 3.0 %collective-permute-done.2.other_data = f32[256,128]{1,0:T(8,128)S(1)} collective-permute-done((f32[256,128]{1,0:T(8,128)S(1)}, f32[256,128]{1,0:T(8,128)S(1)}, u32[]{:S(2)}, u32[]{:S(2)}) %collective-permute-start.2) | collective-permute-done | bytes 131104 | tf_op jit(solution)/shard_map/ppermute | solution.py:174
  29.8 1.4 %shard_map.81 = (f32[256,128]{1,0:T(8,128)}, f32[256,128]{1,0:T(8,128)S(1)}) custom-call(f32[256,128]{1,0:T(8,128)S(1)} %get-tuple-element.18.data, f32[256,128]{1,0:T(8,128)S(1)} %collective-permute-done.2.other_data, f32[256,256]{1,0:T(8,128)S(1)} %get-tuple-element.20.schur, f32[256,256]{1,0:T(8,128)S(1)} %get-tuple-element.21.inverse, ...), custom_call_target="tpu_custom_call" | custom-call | flops 134217728 | bytes 1179648 | tf_op jit(solution)/shard_map/pallas_call | solution.py:157
  31.2 0.8 %collective-permute-start.3 = (f32[256,128]{1,0:T(8,128)S(1)}, f32[256,128]{1,0:T(8,128)S(1)}, u32[]{:S(2)}, u32[]{:S(2)}) collective-permute-start(f32[256,128]{1,0:T(8,128)S(1)} %get-tuple-element.25), channel_id=1, source_target_pairs={{0,8},{8,0},{4,12},{12,4},{16,24},{24,16},{20,28},{28,20},{1,9},{9... | collective-permute-start | bytes 393224 | tf_op jit(solution)/shard_map/ppermute | solution.py:174
  32.0 4.2 %collective-permute-done.3 = f32[256,128]{1,0:T(8,128)S(1)} collective-permute-done((f32[256,128]{1,0:T(8,128)S(1)}, f32[256,128]{1,0:T(8,128)S(1)}, u32[]{:S(2)}, u32[]{:S(2)}) %collective-permute-start.3) | collective-permute-done | bytes 131104 | tf_op jit(solution)/shard_map/ppermute | solution.py:174
  36.2 0.7 %maximum_bitcast_fusion = f32[1,1,512,128]{3,2,1,0:T(8,128)} fusion(f32[256,128]{1,0:T(8,128)S(1)} %get-tuple-element.27, f32[256,128]{1,0:T(8,128)S(1)} %get-tuple-element.26), kind=kLoop, calls=%fused_computation | loop fusion | flops 65536 | bytes 524288 | tf_op jit(solution)/shard_map/broadcast_in_dim | solution.py:380
  (1 shorter events, 0.0 us)
Async XLA Ops:
  0.6 7.9 %copy-start.1 = (bf16[1,3,8,16,16,128]{5,4,3,2,1,0:T(8,128)(2,1)S(1)}, bf16[1,3,8,16,16,128]{5,4,3,2,1,0:T(8,128)(2,1)}, u32[]{:S(2)}) copy-start(bf16[1,3,8,16,16,128]{5,4,3,2,1,0:T(8,128)(2,1)} %param.6) | copy-start | bytes 4718596
  0.6 7.9 %copy-start = (bf16[1,1,512,2048]{3,2,1,0:T(8,128)(2,1)S(1)}, bf16[1,1,512,2048]{3,2,1,0:T(8,128)(2,1)}, u32[]{:S(2)}) copy-start(bf16[1,1,512,2048]{3,2,1,0:T(8,128)(2,1)} %param.10) | copy-start | bytes 6291460
  0.6 3.0 %collective-permute-start = (f32[512,512]{1,0:T(8,128)}, f32[512,512]{1,0:T(8,128)S(1)}, u32[]{:S(2)}, u32[]{:S(2)}) collective-permute-start(f32[512,512]{1,0:T(8,128)} %bitcast.11), channel_id=1, source_target_pairs={{0,4},{4,0},{8,12},{12,8},{16,20},{20,16},{24,28},{28,24},{1,5},{5... | collective-permute-start | bytes 3145736 | tf_op jit(solution)/shard_map/ppermute | solution.py:174
  3.7 1.2 %copy-start.2 = (f32[1,1,512,512]{3,2,1,0:T(8,128)S(1)}, f32[1,1,512,512]{3,2,1,0:T(8,128)}, u32[]{:S(2)}) copy-start(f32[1,1,512,512]{3,2,1,0:T(8,128)} %param.11) | copy-start | bytes 3145732
  4.9 3.7 %copy-start.5 = (f32[1,8,16,16]{3,2,1,0:T(8,128)S(1)}, f32[1,8,16,16]{3,2,1,0:T(8,128)}, u32[]{:S(2)}) copy-start(f32[1,8,16,16]{3,2,1,0:T(8,128)} %param.8) | copy-start | bytes 24580
  8.6 0.9 %copy-start.4 = (f32[1,3,8,16,16]{4,3,2,1,0:T(8,128)S(1)}, f32[1,3,8,16,16]{4,3,2,1,0:T(8,128)}, u32[]{:S(2)}) copy-start(f32[1,3,8,16,16]{4,3,2,1,0:T(8,128)} %param.7) | copy-start | bytes 73732
  9.5 0.8 %copy-start.6 = (s32[1,8,16,16]{3,2,1,0:T(8,128)S(1)}, s32[1,8,16,16]{3,2,1,0:T(8,128)}, u32[]{:S(2)}) copy-start(s32[1,8,16,16]{3,2,1,0:T(8,128)} %param.9) | copy-start | bytes 24580
  10.3 12.9 %copy-start.3 = (f32[1,1,512,512]{3,2,1,0:T(8,128)S(1)}, f32[1,1,512,512]{3,2,1,0:T(8,128)}, u32[]{:S(2)}) copy-start(f32[1,1,512,512]{3,2,1,0:T(8,128)} %param.11) | copy-start | bytes 3145732
  21.6 1.6 %collective-permute-start.1 = (f32[512,128]{1,0:T(8,128)S(1)}, f32[512,128]{1,0:T(8,128)S(1)}, u32[]{:S(2)}, u32[]{:S(2)}) collective-permute-start(f32[512,128]{1,0:T(8,128)S(1)} %get-tuple-element.15.data), channel_id=1, source_target_pairs={{0,4},{4,0},{8,12},{12,8},{16,20},{20,16},{24,28},{28,24},{1,5},{5... | collective-permute-start | bytes 786440 | tf_op jit(solution)/shard_map/ppermute | solution.py:174
  24.2 5.6 %collective-permute-start.2 = (f32[256,128]{1,0:T(8,128)S(1)}, f32[256,128]{1,0:T(8,128)S(1)}, u32[]{:S(2)}, u32[]{:S(2)}) collective-permute-start(f32[256,128]{1,0:T(8,128)S(1)} %get-tuple-element.18.data), channel_id=1, source_target_pairs={{0,8},{8,0},{4,12},{12,4},{16,24},{24,16},{20,28},{28,20},{1,9},{9... | collective-permute-start | bytes 393224 | tf_op jit(solution)/shard_map/ppermute | solution.py:174
  31.2 5.0 %collective-permute-start.3 = (f32[256,128]{1,0:T(8,128)S(1)}, f32[256,128]{1,0:T(8,128)S(1)}, u32[]{:S(2)}, u32[]{:S(2)}) collective-permute-start(f32[256,128]{1,0:T(8,128)S(1)} %get-tuple-element.25), channel_id=1, source_target_pairs={{0,8},{8,0},{4,12},{12,4},{16,24},{24,16},{20,28},{28,20},{1,9},{9... | collective-permute-start | bytes 393224 | tf_op jit(solution)/shard_map/ppermute | solution.py:174

commit v4 on v3

--- a/solution.py
+++ b/solution.py
@@ -200,6 +200,16 @@
     def _():
         pl.semaphore_signal(barrier, inc=1, device_id={"slab": upper}, device_id_type=MESH)
 
+    pl.semaphore_wait(barrier, 1 + has_low.astype(jnp.int32) + has_high.astype(jnp.int32))
+    swap = pltpu.make_async_remote_copy(
+        src_ref=parent,
+        dst_ref=other_parent,
+        send_sem=send_sem.at[2],
+        recv_sem=receive_sem.at[2],
+        device_id={"box": across_box},
+        device_id_type=MESH,
+    )
+    swap.start()
     sizex, sizey, depth, snaps = part.shape
     plane = (sizey, depth, snaps)
     at_z = lax.broadcasted_iota(jnp.int32, plane, 1)
@@ -232,7 +242,6 @@
     for i in range(4):
         loads[i].wait()
     lax.fori_loop(0, sizex, current, 0)
-    pl.semaphore_wait(barrier, 1 + has_low.astype(jnp.int32) + has_high.astype(jnp.int32))
     down = pltpu.make_async_remote_copy(
         src_ref=ends.at[0],
         dst_ref=high_halo,
@@ -250,15 +259,6 @@
         device_id_type=MESH,
     )
 
-    swap = pltpu.make_async_remote_copy(
-        src_ref=parent,
-        dst_ref=other_parent,
-        send_sem=send_sem.at[2],
-        recv_sem=receive_sem.at[2],
-        device_id={"box": across_box},
-        device_id_type=MESH,
-    )
-
     @pl.when(has_low)
     def _():
         down.start()
@@ -274,8 +274,6 @@
     @pl.when(jnp.logical_not(has_high))
     def _():
         high_halo[...] = jnp.zeros_like(high_halo)
-
-    swap.start()
 
     def along(x, carry):
         part[x] += flow_x[x + 2] - flow_x[x]

time: 37.6 us -> 37.4 us (level); the launches traced: 36.9 us -> 37.2 us
  starting transfers between devices: 2.28 us -> 0.95 us
  waiting for transfers between devices: 11.2 us -> 12.5 us
    ppermute x4, starting transfers between devices: 2.28 us -> 0.95 us  [from_partner(): return lax.ppermute(block, axis, route)]
    ppermute x4, waiting for transfers between devices: 11.2 us -> 12.5 us  [from_partner(): return lax.ppermute(block, axis, route)]
    pallas_call x1, Pallas kernels: 11.3 us -> 12.4 us  [front(): pl.pallas_call(front_kernel, out_shape=[jax.ShapeDtypeStruct((solution_ma...]
    pallas_call x4, Pallas kernels: 7.74 us -> 6.92 us  [local(): pl.pallas_call(kernel, out_shape=[jax.ShapeDtypeStruct(s, jnp.float32) fo...]
where the time goes in v4:
time: 37.4 us; the launch traced here: 37.2 us
  Pallas kernels  19.3 us (52%)
  waiting for transfers between devices  12.5 us (33%)
  local copies, waits for them, and re-layouts  3 us (8%)
  starting transfers between devices  0.95 us (3%)
  other arithmetic  0.74 us (2%)
  between operations  0.73 us (2%)
    ppermute x4, waiting for transfers between devices, from_partner(): return lax.ppermute(block, axis, route)  12.5 us
    pallas_call x1, Pallas kernels, front(): pl.pallas_call(front_kernel, out_shape=[jax.ShapeDtypeStruct((solution_ma...  12.4 us
    pallas_call x4, Pallas kernels, local(): pl.pallas_call(kernel, out_shape=[jax.ShapeDtypeStruct(s, jnp.float32) fo...  6.92 us
    unnamed x14, local copies, waits for them, and re-layouts  3 us
    ppermute x4, starting transfers between devices, from_partner(): return lax.ppermute(block, axis, route)  0.95 us
  transfers between devices with their start and end apart: 4, of which 4 were waited for; matrix products, arithmetic and copies ran while one was open for 0% of the time, Pallas kernels for 5%

profile of v4, /device:TPU:0, one launch (start us, length us, event | category | flops | bytes accessed | tf_op | source)
XLA Modules:
  0.0 37.2 jit_solution(14032779969286033980)
XLA Ops:
  0.6 0.0 copy-start.1
  0.6 0.0 copy-start
  0.6 0.5 %collective-permute-start = (f32[512,512]{1,0:T(8,128)}, f32[512,512]{1,0:T(8,128)S(1)}, u32[]{:S(2)}, u32[]{:S(2)}) collective-permute-start(f32[512,512]{1,0:T(8,128)} %bitcast.11), channel_id=1, source_target_pairs={{0,4},{4,0},{8,12},{12,8},{16,20},{20,16},{24,28},{28,24},{1,5},{5... | collective-permute-start | bytes 3145736 | tf_op jit(solution)/shard_map/ppermute | solution.py:174
  1.2 2.5 %collective-permute-done.other = f32[512,512]{1,0:T(8,128)S(1)} collective-permute-done((f32[512,512]{1,0:T(8,128)}, f32[512,512]{1,0:T(8,128)S(1)}, u32[]{:S(2)}, u32[]{:S(2)}) %collective-permute-start) | collective-permute-done | bytes 1048608 | tf_op jit(solution)/shard_map/ppermute | solution.py:174
  3.7 0.0 copy-start.2
  3.7 1.2 %copy-done.2 = f32[1,1,512,512]{3,2,1,0:T(8,128)S(1)} copy-done((f32[1,1,512,512]{3,2,1,0:T(8,128)S(1)}, f32[1,1,512,512]{3,2,1,0:T(8,128)}, u32[]{:S(2)}) %copy-start.2) | copy-done | bytes 1048600
  4.9 0.0 copy-start.5
  4.9 2.8 %shard_map.77 = (f32[256,256]{1,0:T(8,128)S(1)}, f32[256,256]{1,0:T(8,128)S(1)}, f32[256,256]{1,0:T(8,128)S(1)}, f32[256,256]{1,0:T(8,128)S(1)}) custom-call(f32[512,512]{1,0:T(8,128)S(1)} %bitcast.12, f32[512,512]{1,0:T(8,128)S(1)} %collective-permute-done.other), custom_call_target="tpu_custom_call" | custom-call | flops 1006632960 | bytes 2097152 | tf_op jit(solution)/shard_map/pallas_call | solution.py:157
  7.7 0.0 copy-done.1
  7.7 0.0 copy-done
  7.7 0.0 copy-done.5
  7.7 0.0 copy-start.4
  7.8 0.9 %copy-done.4 = f32[1,3,8,16,16]{4,3,2,1,0:T(8,128)S(1)} copy-done((f32[1,3,8,16,16]{4,3,2,1,0:T(8,128)S(1)}, f32[1,3,8,16,16]{4,3,2,1,0:T(8,128)}, u32[]{:S(2)}) %copy-start.4) | copy-done | bytes 24600
  8.7 0.0 copy-start.6
  8.7 0.8 %copy-done.6 = s32[1,8,16,16]{3,2,1,0:T(8,128)S(1)} copy-done((s32[1,8,16,16]{3,2,1,0:T(8,128)S(1)}, s32[1,8,16,16]{3,2,1,0:T(8,128)}, u32[]{:S(2)}) %copy-start.6) | copy-done | bytes 8216
  9.5 0.0 copy-start.3
  9.5 12.4 %shard_map.78 = (f32[512,128]{1,0:T(8,128)S(1)}, f32[256,256]{1,0:T(8,128)S(1)}) custom-call(bf16[3,8,16,16,128]{4,3,2,1,0:T(8,128)(2,1)S(1)} %bitcast.10, f32[3,8,16,16]{3,2,1,0:T(8,128)S(1)} %bitcast.14, f32[8,16,16]{2,1,0:T(8,128)S(1)} %bitcast.15, s32[8,16,16]{2,1,0:T(8,128)S(1)} %bitcast.16, bf16[512,2048]{1,0:T(8,128)(2,1)S(1)} %bitcast.9, ...), custom_call_target="tpu_custom_call" | custom-call | flops 268435456 | bytes 4194304 | tf_op jit(solution)/shard_map/pallas_call | solution.py:313
  21.9 0.1 collective-permute-start.1
  21.9 1.5 %collective-permute-done.1.other_data = f32[512,128]{1,0:T(8,128)S(1)} collective-permute-done((f32[512,128]{1,0:T(8,128)S(1)}, f32[512,128]{1,0:T(8,128)S(1)}, u32[]{:S(2)}, u32[]{:S(2)}) %collective-permute-start.1) | collective-permute-done | bytes 262176 | tf_op jit(solution)/shard_map/ppermute | solution.py:174
  23.5 0.0 copy-done.3
  23.5 1.0 %shard_map.79 = (f32[256,128]{1,0:T(8,128)S(1)}, f32[256,128]{1,0:T(8,128)S(1)}) custom-call(f32[512,512]{1,0:T(8,128)S(1)} %bitcast.13, f32[512,512]{1,0:T(8,128)S(1)} %collective-permute-done.other, f32[512,128]{1,0:T(8,128)S(1)} %get-tuple-element.15.data, f32[512,128]{1,0:T(8,128)S(1)} %collective-permute-done.1.other_data, ...), custom_call_target="tpu_custom_call" | custom-call | flops 201326592 | bytes 3145728 | tf_op jit(solution)/shard_map/pallas_call | solution.py:157
  24.5 0.1 collective-permute-start.2
  24.5 1.7 %shard_map.80 = (f32[256,256]{1,0:T(8,128)S(1)}, f32[256,256]{1,0:T(8,128)S(1)}) custom-call(f32[256,256]{1,0:T(8,128)S(1)} %get-tuple-element.14.refs_5_.parent, f32[256,256]{1,0:T(8,128)S(1)} %get-tuple-element.19.other_parent), custom_call_target="tpu_custom_call" | custom-call | flops 671088640 | bytes 524288 | tf_op jit(solution)/shard_map/pallas_call | solution.py:157
  26.3 3.8 %collective-permute-done.2.other_data = f32[256,128]{1,0:T(8,128)S(1)} collective-permute-done((f32[256,128]{1,0:T(8,128)S(1)}, f32[256,128]{1,0:T(8,128)S(1)}, u32[]{:S(2)}, u32[]{:S(2)}) %collective-permute-start.2) | collective-permute-done | bytes 131104 | tf_op jit(solution)/shard_map/ppermute | solution.py:174
  30.1 1.4 %shard_map.81 = (f32[256,128]{1,0:T(8,128)}, f32[256,128]{1,0:T(8,128)S(1)}) custom-call(f32[256,128]{1,0:T(8,128)S(1)} %get-tuple-element.18.data, f32[256,128]{1,0:T(8,128)S(1)} %collective-permute-done.2.other_data, f32[256,256]{1,0:T(8,128)S(1)} %get-tuple-element.20.schur, f32[256,256]{1,0:T(8,128)S(1)} %get-tuple-element.21.inverse, ...), custom_call_target="tpu_custom_call" | custom-call | flops 134217728 | bytes 1179648 | tf_op jit(solution)/shard_map/pallas_call | solution.py:157
  31.5 0.3 collective-permute-start.3
  31.7 4.7 %collective-permute-done.3 = f32[256,128]{1,0:T(8,128)S(1)} collective-permute-done((f32[256,128]{1,0:T(8,128)S(1)}, f32[256,128]{1,0:T(8,128)S(1)}, u32[]{:S(2)}, u32[]{:S(2)}) %collective-permute-start.3) | collective-permute-done | bytes 131104 | tf_op jit(solution)/shard_map/ppermute | solution.py:174
  36.5 0.7 %maximum_bitcast_fusion = f32[1,1,512,128]{3,2,1,0:T(8,128)} fusion(f32[256,128]{1,0:T(8,128)S(1)} %get-tuple-element.27, f32[256,128]{1,0:T(8,128)S(1)} %get-tuple-element.26), kind=kLoop, calls=%fused_computation | loop fusion | flops 65536 | bytes 524288 | tf_op jit(solution)/shard_map/broadcast_in_dim | solution.py:378
  (1 shorter events, 0.0 us)
Async XLA Ops:
  0.6 7.1 %copy-start.1 = (bf16[1,3,8,16,16,128]{5,4,3,2,1,0:T(8,128)(2,1)S(1)}, bf16[1,3,8,16,16,128]{5,4,3,2,1,0:T(8,128)(2,1)}, u32[]{:S(2)}) copy-start(bf16[1,3,8,16,16,128]{5,4,3,2,1,0:T(8,128)(2,1)} %param.6) | copy-start | bytes 4718596
  0.6 7.1 %copy-start = (bf16[1,1,512,2048]{3,2,1,0:T(8,128)(2,1)S(1)}, bf16[1,1,512,2048]{3,2,1,0:T(8,128)(2,1)}, u32[]{:S(2)}) copy-start(bf16[1,1,512,2048]{3,2,1,0:T(8,128)(2,1)} %param.10) | copy-start | bytes 6291460
  0.6 3.0 %collective-permute-start = (f32[512,512]{1,0:T(8,128)}, f32[512,512]{1,0:T(8,128)S(1)}, u32[]{:S(2)}, u32[]{:S(2)}) collective-permute-start(f32[512,512]{1,0:T(8,128)} %bitcast.11), channel_id=1, source_target_pairs={{0,4},{4,0},{8,12},{12,8},{16,20},{20,16},{24,28},{28,24},{1,5},{5... | collective-permute-start | bytes 3145736 | tf_op jit(solution)/shard_map/ppermute | solution.py:174
  3.7 1.2 %copy-start.2 = (f32[1,1,512,512]{3,2,1,0:T(8,128)S(1)}, f32[1,1,512,512]{3,2,1,0:T(8,128)}, u32[]{:S(2)}) copy-start(f32[1,1,512,512]{3,2,1,0:T(8,128)} %param.11) | copy-start | bytes 3145732
  4.9 2.8 %copy-start.5 = (f32[1,8,16,16]{3,2,1,0:T(8,128)S(1)}, f32[1,8,16,16]{3,2,1,0:T(8,128)}, u32[]{:S(2)}) copy-start(f32[1,8,16,16]{3,2,1,0:T(8,128)} %param.8) | copy-start | bytes 24580
  7.7 0.9 %copy-start.4 = (f32[1,3,8,16,16]{4,3,2,1,0:T(8,128)S(1)}, f32[1,3,8,16,16]{4,3,2,1,0:T(8,128)}, u32[]{:S(2)}) copy-start(f32[1,3,8,16,16]{4,3,2,1,0:T(8,128)} %param.7) | copy-start | bytes 73732
  8.7 0.8 %copy-start.6 = (s32[1,8,16,16]{3,2,1,0:T(8,128)S(1)}, s32[1,8,16,16]{3,2,1,0:T(8,128)}, u32[]{:S(2)}) copy-start(s32[1,8,16,16]{3,2,1,0:T(8,128)} %param.9) | copy-start | bytes 24580
  9.5 14.0 %copy-start.3 = (f32[1,1,512,512]{3,2,1,0:T(8,128)S(1)}, f32[1,1,512,512]{3,2,1,0:T(8,128)}, u32[]{:S(2)}) copy-start(f32[1,1,512,512]{3,2,1,0:T(8,128)} %param.11) | copy-start | bytes 3145732
  21.9 1.6 %collective-permute-start.1 = (f32[512,128]{1,0:T(8,128)S(1)}, f32[512,128]{1,0:T(8,128)S(1)}, u32[]{:S(2)}, u32[]{:S(2)}) collective-permute-start(f32[512,128]{1,0:T(8,128)S(1)} %get-tuple-element.15.data), channel_id=1, source_target_pairs={{0,4},{4,0},{8,12},{12,8},{16,20},{20,16},{24,28},{28,24},{1,5},{5... | collective-permute-start | bytes 786440 | tf_op jit(solution)/shard_map/ppermute | solution.py:174
  24.5 5.6 %collective-permute-start.2 = (f32[256,128]{1,0:T(8,128)S(1)}, f32[256,128]{1,0:T(8,128)S(1)}, u32[]{:S(2)}, u32[]{:S(2)}) collective-permute-start(f32[256,128]{1,0:T(8,128)S(1)} %get-tuple-element.18.data), channel_id=1, source_target_pairs={{0,8},{8,0},{4,12},{12,4},{16,24},{24,16},{20,28},{28,20},{1,9},{9... | collective-permute-start | bytes 393224 | tf_op jit(solution)/shard_map/ppermute | solution.py:174
  31.5 5.0 %collective-permute-start.3 = (f32[256,128]{1,0:T(8,128)S(1)}, f32[256,128]{1,0:T(8,128)S(1)}, u32[]{:S(2)}, u32[]{:S(2)}) collective-permute-start(f32[256,128]{1,0:T(8,128)S(1)} %get-tuple-element.25), channel_id=1, source_target_pairs={{0,8},{8,0},{4,12},{12,4},{16,24},{24,16},{20,28},{28,20},{1,9},{9... | collective-permute-start | bytes 393224 | tf_op jit(solution)/shard_map/ppermute | solution.py:174

commit v5 on v4

--- a/solution.py
+++ b/solution.py
@@ -190,7 +190,12 @@
     box = lax.axis_index("box")
     across_box = box + 2 - 4 * lax.rem(lax.div(box, 2), 2)
     barrier = pltpu.get_barrier_semaphore()
+    core = lax.rem(box, 2)
+    beside = box + 1 - 2 * core
+    share = parent.shape[0] // 2
+    mine = pl.ds(pl.multiple_of(core * share, share), share)
     pl.semaphore_signal(barrier, inc=1, device_id={"box": across_box}, device_id_type=MESH)
+    pl.semaphore_signal(barrier, inc=1, device_id={"box": beside}, device_id_type=MESH)
 
     @pl.when(has_low)
     def _():
@@ -200,10 +205,10 @@
     def _():
         pl.semaphore_signal(barrier, inc=1, device_id={"slab": upper}, device_id_type=MESH)
 
-    pl.semaphore_wait(barrier, 1 + has_low.astype(jnp.int32) + has_high.astype(jnp.int32))
+    pl.semaphore_wait(barrier, 2 + has_low.astype(jnp.int32) + has_high.astype(jnp.int32))
     swap = pltpu.make_async_remote_copy(
-        src_ref=parent,
-        dst_ref=other_parent,
+        src_ref=parent.at[mine],
+        dst_ref=other_parent.at[mine],
         send_sem=send_sem.at[2],
         recv_sem=receive_sem.at[2],
         device_id={"box": across_box},
@@ -301,9 +306,19 @@
         return carry
 
     lax.fori_loop(0, sizex, finish, 0)
+    swap.wait()
+    relay = pltpu.make_async_remote_copy(
+        src_ref=other_parent.at[mine],
+        dst_ref=other_parent.at[mine],
+        send_sem=send_sem.at[3],
+        recv_sem=receive_sem.at[3],
+        device_id={"box": beside},
+        device_id_type=MESH,
+    )
+    relay.start()
     loads[4].wait()
     neumann[...] = jnp.dot(solution_map[...], source[...], preferred_element_type=jnp.float32)
-    swap.wait()
+    relay.wait()
 
 
 def front(velocity, field, conductivity, wall_flags, solution_map, parent):
@@ -326,8 +341,8 @@
             pltpu.VMEM((sizex, sizey, 1, snaps), f32),
             pltpu.VMEM((sizex, sizey, 1, snaps), f32),
             pltpu.VMEM((sizex * sizey * depth, snaps), jnp.bfloat16),
-            pltpu.SemaphoreType.DMA((3,)),
-            pltpu.SemaphoreType.DMA((3,)),
+            pltpu.SemaphoreType.DMA((4,)),
+            pltpu.SemaphoreType.DMA((4,)),
             pltpu.SemaphoreType.DMA((5,)),
         ],
         compiler_params=pltpu.CompilerParams(

time: 37.4 us -> 36.6 us (0.979)
  waiting for transfers between devices: 12.5 us -> 8.83 us
  starting transfers between devices: 0.95 us -> 4 us
    ppermute x4, waiting for transfers between devices: 12.5 us -> 8.83 us  [from_partner(): return lax.ppermute(block, axis, route)]
    ppermute x4, starting transfers between devices: 0.95 us -> 4 us  [from_partner(): return lax.ppermute(block, axis, route)]
    pallas_call x1, Pallas kernels: 12.4 us -> 11.4 us  [front(): pl.pallas_call(front_kernel, out_shape=[jax.ShapeDtypeStruct((solution_ma...]
    pallas_call x4, Pallas kernels: 6.92 us -> 7.75 us  [local(): pl.pallas_call(kernel, out_shape=[jax.ShapeDtypeStruct(s, jnp.float32) fo...]
  transfers between devices with their start and end apart: 4 -> 4, of which waited for: 4 -> 4; matrix products, arithmetic and copies ran while one was open for 0% -> 0% of each run, Pallas kernels for 5% -> 7%
where the time goes in v5:
time: 36.6 us; the launch traced here: 36.4 us
  Pallas kernels  19.1 us (52%)
  waiting for transfers between devices  8.83 us (24%)
  starting transfers between devices  4 us (11%)
  local copies, waits for them, and re-layouts  3 us (8%)
  other arithmetic  0.74 us (2%)
  between operations  0.72 us (2%)
    pallas_call x1, Pallas kernels, front(): pl.pallas_call(front_kernel, out_shape=[jax.ShapeDtypeStruct((solution_ma...  11.4 us
    ppermute x4, waiting for transfers between devices, from_partner(): return lax.ppermute(block, axis, route)  8.83 us
    pallas_call x4, Pallas kernels, local(): pl.pallas_call(kernel, out_shape=[jax.ShapeDtypeStruct(s, jnp.float32) fo...  7.75 us
    ppermute x4, starting transfers between devices, from_partner(): return lax.ppermute(block, axis, route)  4 us
    unnamed x14, local copies, waits for them, and re-layouts  3 us
  transfers between devices with their start and end apart: 4, of which 4 were waited for; matrix products, arithmetic and copies ran while one was open for 0% of the time, Pallas kernels for 7%

profile of v5, /device:TPU:0, one launch (start us, length us, event | category | flops | bytes accessed | tf_op | source)
XLA Modules:
  0.0 36.4 jit_solution(1374093523662495414)
XLA Ops:
  0.6 0.0 copy-start.1
  0.6 0.0 copy-start
  0.6 0.5 %collective-permute-start = (f32[512,512]{1,0:T(8,128)}, f32[512,512]{1,0:T(8,128)S(1)}, u32[]{:S(2)}, u32[]{:S(2)}) collective-permute-start(f32[512,512]{1,0:T(8,128)} %bitcast.11), channel_id=1, source_target_pairs={{0,4},{4,0},{8,12},{12,8},{16,20},{20,16},{24,28},{28,24},{1,5},{5... | collective-permute-start | bytes 3145736 | tf_op jit(solution)/shard_map/ppermute | solution.py:174
  1.2 2.5 %collective-permute-done.other = f32[512,512]{1,0:T(8,128)S(1)} collective-permute-done((f32[512,512]{1,0:T(8,128)}, f32[512,512]{1,0:T(8,128)S(1)}, u32[]{:S(2)}, u32[]{:S(2)}) %collective-permute-start) | collective-permute-done | bytes 1048608 | tf_op jit(solution)/shard_map/ppermute | solution.py:174
  3.7 0.0 copy-start.2
  3.7 1.2 %copy-done.2 = f32[1,1,512,512]{3,2,1,0:T(8,128)S(1)} copy-done((f32[1,1,512,512]{3,2,1,0:T(8,128)S(1)}, f32[1,1,512,512]{3,2,1,0:T(8,128)}, u32[]{:S(2)}) %copy-start.2) | copy-done | bytes 1048600
  4.9 0.0 copy-start.5
  4.9 2.8 %shard_map.77 = (f32[256,256]{1,0:T(8,128)S(1)}, f32[256,256]{1,0:T(8,128)S(1)}, f32[256,256]{1,0:T(8,128)S(1)}, f32[256,256]{1,0:T(8,128)S(1)}) custom-call(f32[512,512]{1,0:T(8,128)S(1)} %bitcast.12, f32[512,512]{1,0:T(8,128)S(1)} %collective-permute-done.other), custom_call_target="tpu_custom_call" | custom-call | flops 1006632960 | bytes 2097152 | tf_op jit(solution)/shard_map/pallas_call | solution.py:157
  7.7 0.0 copy-done.1
  7.7 0.0 copy-done
  7.7 0.0 copy-done.5
  7.7 0.0 copy-start.4
  7.8 0.9 %copy-done.4 = f32[1,3,8,16,16]{4,3,2,1,0:T(8,128)S(1)} copy-done((f32[1,3,8,16,16]{4,3,2,1,0:T(8,128)S(1)}, f32[1,3,8,16,16]{4,3,2,1,0:T(8,128)}, u32[]{:S(2)}) %copy-start.4) | copy-done | bytes 24600
  8.7 0.0 copy-start.6
  8.7 0.8 %copy-done.6 = s32[1,8,16,16]{3,2,1,0:T(8,128)S(1)} copy-done((s32[1,8,16,16]{3,2,1,0:T(8,128)S(1)}, s32[1,8,16,16]{3,2,1,0:T(8,128)}, u32[]{:S(2)}) %copy-start.6) | copy-done | bytes 8216
  9.5 0.0 copy-start.3
  9.5 11.4 %shard_map.78 = (f32[512,128]{1,0:T(8,128)S(1)}, f32[256,256]{1,0:T(8,128)S(1)}) custom-call(bf16[3,8,16,16,128]{4,3,2,1,0:T(8,128)(2,1)S(1)} %bitcast.10, f32[3,8,16,16]{3,2,1,0:T(8,128)S(1)} %bitcast.14, f32[8,16,16]{2,1,0:T(8,128)S(1)} %bitcast.15, s32[8,16,16]{2,1,0:T(8,128)S(1)} %bitcast.16, bf16[512,2048]{1,0:T(8,128)(2,1)S(1)} %bitcast.9, ...), custom_call_target="tpu_custom_call" | custom-call | flops 268435456 | bytes 4194304 | tf_op jit(solution)/shard_map/pallas_call | solution.py:328
  20.9 0.4 %collective-permute-start.1 = (f32[512,128]{1,0:T(8,128)S(1)}, f32[512,128]{1,0:T(8,128)S(1)}, u32[]{:S(2)}, u32[]{:S(2)}) collective-permute-start(f32[512,128]{1,0:T(8,128)S(1)} %get-tuple-element.15.data), channel_id=1, source_target_pairs={{0,4},{4,0},{8,12},{12,8},{16,20},{20,16},{24,28},{28,24},{1,5},{5... | collective-permute-start | bytes 786440 | tf_op jit(solution)/shard_map/ppermute | solution.py:174
  21.3 1.2 %collective-permute-done.1.other_data = f32[512,128]{1,0:T(8,128)S(1)} collective-permute-done((f32[512,128]{1,0:T(8,128)S(1)}, f32[512,128]{1,0:T(8,128)S(1)}, u32[]{:S(2)}, u32[]{:S(2)}) %collective-permute-start.1) | collective-permute-done | bytes 262176 | tf_op jit(solution)/shard_map/ppermute | solution.py:174
  22.5 0.0 copy-done.3
  22.5 1.0 %shard_map.79 = (f32[256,128]{1,0:T(8,128)S(1)}, f32[256,128]{1,0:T(8,128)S(1)}) custom-call(f32[512,512]{1,0:T(8,128)S(1)} %bitcast.13, f32[512,512]{1,0:T(8,128)S(1)} %collective-permute-done.other, f32[512,128]{1,0:T(8,128)S(1)} %get-tuple-element.15.data, f32[512,128]{1,0:T(8,128)S(1)} %collective-permute-done.1.other_data, ...), custom_call_target="tpu_custom_call" | custom-call | flops 201326592 | bytes 3145728 | tf_op jit(solution)/shard_map/pallas_call | solution.py:157
  23.5 1.6 %collective-permute-start.2 = (f32[256,128]{1,0:T(8,128)S(1)}, f32[256,128]{1,0:T(8,128)S(1)}, u32[]{:S(2)}, u32[]{:S(2)}) collective-permute-start(f32[256,128]{1,0:T(8,128)S(1)} %get-tuple-element.18.data), channel_id=1, source_target_pairs={{0,8},{8,0},{4,12},{12,4},{16,24},{24,16},{20,28},{28,20},{1,9},{9... | collective-permute-start | bytes 393224 | tf_op jit(solution)/shard_map/ppermute | solution.py:174
  25.1 2.6 %shard_map.80 = (f32[256,256]{1,0:T(8,128)S(1)}, f32[256,256]{1,0:T(8,128)S(1)}) custom-call(f32[256,256]{1,0:T(8,128)S(1)} %get-tuple-element.14.refs_5_.parent, f32[256,256]{1,0:T(8,128)S(1)} %get-tuple-element.19.other_parent), custom_call_target="tpu_custom_call" | custom-call | flops 671088640 | bytes 524288 | tf_op jit(solution)/shard_map/pallas_call | solution.py:157
  27.7 1.7 %collective-permute-done.2.other_data = f32[256,128]{1,0:T(8,128)S(1)} collective-permute-done((f32[256,128]{1,0:T(8,128)S(1)}, f32[256,128]{1,0:T(8,128)S(1)}, u32[]{:S(2)}, u32[]{:S(2)}) %collective-permute-start.2) | collective-permute-done | bytes 131104 | tf_op jit(solution)/shard_map/ppermute | solution.py:174
  29.3 1.4 %shard_map.81 = (f32[256,128]{1,0:T(8,128)}, f32[256,128]{1,0:T(8,128)S(1)}) custom-call(f32[256,128]{1,0:T(8,128)S(1)} %get-tuple-element.18.data, f32[256,128]{1,0:T(8,128)S(1)} %collective-permute-done.2.other_data, f32[256,256]{1,0:T(8,128)S(1)} %get-tuple-element.20.schur, f32[256,256]{1,0:T(8,128)S(1)} %get-tuple-element.21.inverse, ...), custom_call_target="tpu_custom_call" | custom-call | flops 134217728 | bytes 1179648 | tf_op jit(solution)/shard_map/pallas_call | solution.py:157
  30.7 1.5 %collective-permute-start.3 = (f32[256,128]{1,0:T(8,128)S(1)}, f32[256,128]{1,0:T(8,128)S(1)}, u32[]{:S(2)}, u32[]{:S(2)}) collective-permute-start(f32[256,128]{1,0:T(8,128)S(1)} %get-tuple-element.25), channel_id=1, source_target_pairs={{0,8},{8,0},{4,12},{12,4},{16,24},{24,16},{20,28},{28,20},{1,9},{9... | collective-permute-start | bytes 393224 | tf_op jit(solution)/shard_map/ppermute | solution.py:174
  32.2 3.5 %collective-permute-done.3 = f32[256,128]{1,0:T(8,128)S(1)} collective-permute-done((f32[256,128]{1,0:T(8,128)S(1)}, f32[256,128]{1,0:T(8,128)S(1)}, u32[]{:S(2)}, u32[]{:S(2)}) %collective-permute-start.3) | collective-permute-done | bytes 131104 | tf_op jit(solution)/shard_map/ppermute | solution.py:174
  35.7 0.7 %maximum_bitcast_fusion = f32[1,1,512,128]{3,2,1,0:T(8,128)} fusion(f32[256,128]{1,0:T(8,128)S(1)} %get-tuple-element.27, f32[256,128]{1,0:T(8,128)S(1)} %get-tuple-element.26), kind=kLoop, calls=%fused_computation | loop fusion | flops 65536 | bytes 524288 | tf_op jit(solution)/shard_map/broadcast_in_dim | solution.py:393
  (1 shorter events, 0.0 us)
Async XLA Ops:
  0.6 7.1 %copy-start.1 = (bf16[1,3,8,16,16,128]{5,4,3,2,1,0:T(8,128)(2,1)S(1)}, bf16[1,3,8,16,16,128]{5,4,3,2,1,0:T(8,128)(2,1)}, u32[]{:S(2)}) copy-start(bf16[1,3,8,16,16,128]{5,4,3,2,1,0:T(8,128)(2,1)} %param.6) | copy-start | bytes 4718596
  0.6 7.1 %copy-start = (bf16[1,1,512,2048]{3,2,1,0:T(8,128)(2,1)S(1)}, bf16[1,1,512,2048]{3,2,1,0:T(8,128)(2,1)}, u32[]{:S(2)}) copy-start(bf16[1,1,512,2048]{3,2,1,0:T(8,128)(2,1)} %param.10) | copy-start | bytes 6291460
  0.6 3.0 %collective-permute-start = (f32[512,512]{1,0:T(8,128)}, f32[512,512]{1,0:T(8,128)S(1)}, u32[]{:S(2)}, u32[]{:S(2)}) collective-permute-start(f32[512,512]{1,0:T(8,128)} %bitcast.11), channel_id=1, source_target_pairs={{0,4},{4,0},{8,12},{12,8},{16,20},{20,16},{24,28},{28,24},{1,5},{5... | collective-permute-start | bytes 3145736 | tf_op jit(solution)/shard_map/ppermute | solution.py:174
  3.7 1.2 %copy-start.2 = (f32[1,1,512,512]{3,2,1,0:T(8,128)S(1)}, f32[1,1,512,512]{3,2,1,0:T(8,128)}, u32[]{:S(2)}) copy-start(f32[1,1,512,512]{3,2,1,0:T(8,128)} %param.11) | copy-start | bytes 3145732
  4.9 2.8 %copy-start.5 = (f32[1,8,16,16]{3,2,1,0:T(8,128)S(1)}, f32[1,8,16,16]{3,2,1,0:T(8,128)}, u32[]{:S(2)}) copy-start(f32[1,8,16,16]{3,2,1,0:T(8,128)} %param.8) | copy-start | bytes 24580
  7.7 0.9 %copy-start.4 = (f32[1,3,8,16,16]{4,3,2,1,0:T(8,128)S(1)}, f32[1,3,8,16,16]{4,3,2,1,0:T(8,128)}, u32[]{:S(2)}) copy-start(f32[1,3,8,16,16]{4,3,2,1,0:T(8,128)} %param.7) | copy-start | bytes 73732
  8.7 0.8 %copy-start.6 = (s32[1,8,16,16]{3,2,1,0:T(8,128)S(1)}, s32[1,8,16,16]{3,2,1,0:T(8,128)}, u32[]{:S(2)}) copy-start(s32[1,8,16,16]{3,2,1,0:T(8,128)} %param.9) | copy-start | bytes 24580
  9.5 13.0 %copy-start.3 = (f32[1,1,512,512]{3,2,1,0:T(8,128)S(1)}, f32[1,1,512,512]{3,2,1,0:T(8,128)}, u32[]{:S(2)}) copy-start(f32[1,1,512,512]{3,2,1,0:T(8,128)} %param.11) | copy-start | bytes 3145732
  20.9 1.6 %collective-permute-start.1 = (f32[512,128]{1,0:T(8,128)S(1)}, f32[512,128]{1,0:T(8,128)S(1)}, u32[]{:S(2)}, u32[]{:S(2)}) collective-permute-start(f32[512,128]{1,0:T(8,128)S(1)} %get-tuple-element.15.data), channel_id=1, source_target_pairs={{0,4},{4,0},{8,12},{12,8},{16,20},{20,16},{24,28},{28,24},{1,5},{5... | collective-permute-start | bytes 786440 | tf_op jit(solution)/shard_map/ppermute | solution.py:174
  23.5 5.8 %collective-permute-start.2 = (f32[256,128]{1,0:T(8,128)S(1)}, f32[256,128]{1,0:T(8,128)S(1)}, u32[]{:S(2)}, u32[]{:S(2)}) collective-permute-start(f32[256,128]{1,0:T(8,128)S(1)} %get-tuple-element.18.data), channel_id=1, source_target_pairs={{0,8},{8,0},{4,12},{12,4},{16,24},{24,16},{20,28},{28,20},{1,9},{9... | collective-permute-start | bytes 393224 | tf_op jit(solution)/shard_map/ppermute | solution.py:174
  30.7 5.0 %collective-permute-start.3 = (f32[256,128]{1,0:T(8,128)S(1)}, f32[256,128]{1,0:T(8,128)S(1)}, u32[]{:S(2)}, u32[]{:S(2)}) collective-permute-start(f32[256,128]{1,0:T(8,128)S(1)} %get-tuple-element.25), channel_id=1, source_target_pairs={{0,8},{8,0},{4,12},{12,4},{16,24},{24,16},{20,28},{28,20},{1,9},{9... | collective-permute-start | bytes 393224 | tf_op jit(solution)/shard_map/ppermute | solution.py:174
